TPU v7x, 32 devices: a whole 2x2x4 slice. The times are simulated.
32 devices in a mesh: shard: 4 (over z), ctx: 2 (over core), tp: 4 (over y, x).
Axes of the slice: x: 2, y: 2, z: 4, core: 2. Of those that a mesh axis runs over, the one named last changes fastest.
Arguments:
- hidden: bfloat16 [4, 2048, 1024], P('shard', 'ctx'), may hold values from -6 to 6
- cotangent: bfloat16 [4, 2048, 1024], P('shard', 'ctx'), may hold values from -6 to 6
- lengths: int32 [4], P('shard'), may hold values from 1024 to 2048, as said below
- norm1_gain: bfloat16 [1024], P(('shard', 'ctx')), may hold values from 0.25 to 1.75
- w_z: bfloat16 [1024, 1536], P(('shard', 'ctx'), 'tp'), may hold values from -0.1875 to 0.1875
- w_x: bfloat16 [1024, 1536], P(('shard', 'ctx'), 'tp'), may hold values from -0.1875 to 0.1875
- w_shared: bfloat16 [1024, 512], P(('shard', 'ctx')), may hold values from -0.1875 to 0.1875
- w_dt: bfloat16 [1024, 24], P(('shard', 'ctx')), may hold values from -0.1875 to 0.1875
- dt_bias: bfloat16 [24], replicated, may hold values from -10 to -3
- a_log: bfloat16 [24], replicated, may hold values from -1 to 1
- d_skip: bfloat16 [24], replicated, may hold values from 0.5 to 1.5
- conv_w: bfloat16 [4, 1792], replicated, may hold values from -3 to 3
- conv_b: bfloat16 [1792], replicated, may hold values from -0.5 to 0.5
- gated_gain: bfloat16 [1536], replicated, may hold values from 0.25 to 1.75
- w_out: bfloat16 [1536, 1024], P('tp', ('shard', 'ctx')), may hold values from -0.15625 to 0.15625
- w_q: bfloat16 [1024, 512], P(('shard', 'ctx'), 'tp'), may hold values from -0.1875 to 0.1875
- w_o: bfloat16 [512, 1024], P('tp', ('shard', 'ctx')), may hold values from -2 to 2
- norm2_gain: bfloat16 [1024], P(('shard', 'ctx')), may hold values from 0.25 to 1.75
- w_gate: bfloat16 [1024, 2048], P(('shard', 'ctx'), 'tp'), may hold values from -0.1875 to 0.1875
- w_up: bfloat16 [1024, 2048], P(('shard', 'ctx'), 'tp'), may hold values from -0.1875 to 0.1875
- w_down: bfloat16 [2048, 1024], P('tp', ('shard', 'ctx')), may hold values from -0.125 to 0.125
Outputs:
- output: bfloat16 [4, 2048, 1024], P('shard', 'ctx', 'tp')
- grad_hidden: float32 [4, 2048, 1024], P('shard', 'ctx')
- grad_norm1_gain: float32 [1024], P(('shard', 'ctx', 'tp'))
- grad_w_z: float32 [1024, 1536], P(('shard', 'ctx'), 'tp')
- grad_w_x: float32 [1024, 1536], P(('shard', 'ctx'), 'tp')
- grad_w_shared: float32 [1024, 512], P(('shard', 'ctx', 'tp'))
- grad_w_dt: float32 [1024, 24], P(('shard', 'ctx', 'tp'))
- grad_dt_bias: float32 [24], replicated
- grad_a_log: float32 [24], replicated
- grad_d_skip: float32 [24], replicated
- grad_conv_w: float32 [4, 1792], replicated
- grad_conv_b: float32 [1792], replicated
- grad_gated_gain: float32 [1536], replicated
- grad_w_out: float32 [1536, 1024], P('tp', ('shard', 'ctx'))
- grad_w_q: float32 [1024, 512], P(('shard', 'ctx'), 'tp')
- grad_w_o: float32 [512, 1024], P('tp', ('shard', 'ctx'))
- grad_norm2_gain: float32 [1024], P(('shard', 'ctx', 'tp'))
- grad_w_gate: float32 [1024, 2048], P(('shard', 'ctx'), 'tp')
- grad_w_up: float32 [1024, 2048], P(('shard', 'ctx'), 'tp')
- grad_w_down: float32 [2048, 1024], P('tp', ('shard', 'ctx'))
Inputs may be any that keep to these rules, and one draw needn't show every extreme that they name: `lengths`: each slot holds one sequence from position 0; positions from its length on are padding. In every draw some slot has exactly 2048 positions and another exactly 1024.
All inputs are finite; a program needn't handle non-finite values.
Results may differ from a plain program's by a relative error of at most 0.015.
Values may be sent and summed in bfloat16 or wider, within the bound.
A program may use at most 192 MiB of HBM per device.

v0:
```python
import jax
import jax.numpy as jnp
from jax import lax
from jax.sharding import PartitionSpec as P

H = 24
P_SIZE = 64
N = 128
NQ = 8
KV = 2
HD = 64
CONVW = 4
SCAN_BLOCK = 256
QUERY_BLOCK = 512
DI = 1536


norm_epsilon = 1e-05
rope_base = 10000.0
mask_fill = -1e30
highest = lax.Precision.HIGHEST


def carried_in_2(shard, axis, combine, identity):
    count, mine = (lax.axis_size(axis), lax.axis_index(axis))
    everything = jax.tree.map(
        lambda part, kind: lax.all_gather(part.astype(kind), axis),
        shard,
        (jnp.bfloat16, jnp.bfloat16),
    )
    start = jax.tree.map(
        lambda part, zero: jnp.broadcast_to(jnp.asarray(zero, part.dtype), part.shape),
        shard,
        identity,
    )

    def carried_lap(k, before):
        reached = k < mine
        new = combine(
            before, jax.tree.map(lambda part, own: part[k].astype(own.dtype), everything, shard)
        )
        return jax.tree.map(lambda a, b: jnp.where(reached, a, b), new, before)

    return lax.fori_loop(0, count, carried_lap, start)


def entering(shard, axis, combine, identity):
    count, mine = (lax.axis_size(axis), lax.axis_index(axis))
    everything = jax.tree.map(lambda part: lax.all_gather(part, axis), shard)
    start = jax.tree.map(
        lambda part, zero: jnp.broadcast_to(jnp.asarray(zero, part.dtype), part.shape),
        shard,
        identity,
    )

    def entering_lap(k, before):
        at = count - 1 - k
        reached = at > mine
        new = combine(before, jax.tree.map(lambda part: part[at], everything))
        return jax.tree.map(lambda a, b: jnp.where(reached, a, b), new, before)

    return lax.fori_loop(0, count, entering_lap, start)


def matmul(lhs_matrix, rhs_matrix):
    return jnp.dot(lhs_matrix, rhs_matrix, preferred_element_type=jnp.float32)


def matmul_nt(lhs_matrix, rhs_matrix):
    return lax.dot_general(
        lhs_matrix, rhs_matrix, (((1,), (1,)), ((), ())), preferred_element_type=jnp.float32
    )


def matmul_tn(lhs_matrix, rhs_matrix):
    return lax.dot_general(
        lhs_matrix, rhs_matrix, (((0,), (0,)), ((), ())), preferred_element_type=jnp.float32
    )


def precise_nt(lhs_matrix, rhs_matrix):
    return lax.dot_general(
        lhs_matrix,
        rhs_matrix,
        (((1,), (1,)), ((), ())),
        precision=highest,
        preferred_element_type=jnp.float32,
    )


def precise_tn(lhs_matrix, rhs_matrix):
    return lax.dot_general(
        lhs_matrix,
        rhs_matrix,
        (((0,), (0,)), ((), ())),
        precision=highest,
        preferred_element_type=jnp.float32,
    )


def rotary_tables(positions, width):
    freq_index = jnp.arange(width // 2, dtype=jnp.float32)
    inverse = rope_base ** (-2.0 * freq_index / width)
    angles = positions[:, None] * inverse[None, :]
    angles = jnp.concatenate([angles, angles], axis=-1)
    return (jnp.cos(angles), jnp.sin(angles))


def turn_half(values):
    half_width = values.shape[-1] // 2
    return jnp.concatenate([-values[..., half_width:], values[..., :half_width]], axis=-1)


def rotate(values, cosine, sine):
    return values * cosine + turn_half(values) * sine


def unrotate(values, cosine, sine):
    return values * cosine - turn_half(values) * sine


def causal_conv(inputs, history, kernel, offset):
    padded = jnp.concatenate([history, inputs], axis=1)
    row_count = inputs.shape[1]
    result = offset + jnp.zeros_like(inputs)
    for tap_index in range(kernel.shape[0]):
        result = result + kernel[tap_index] * padded[:, tap_index : tap_index + row_count]
    return result


def state_blocks(values, in_map, out_map, steps, rates, skip, start, block):
    batch_count, row_count, head_count, head_width = values.shape
    block_count = row_count // block
    state_width = in_map.shape[-1]
    value_blocks = values.reshape(batch_count, block_count, block, head_count, head_width)
    in_blocks = in_map.reshape(batch_count, block_count, block, state_width)
    out_blocks = out_map.reshape(batch_count, block_count, block, state_width)
    step_blocks = steps.reshape(batch_count, block_count, block, head_count)
    cumul = jnp.cumsum(rates.reshape(batch_count, block_count, block, head_count), axis=2)
    totals = cumul[:, :, -1, :]
    gram = jnp.einsum("bcin,bcjn->bcij", out_blocks, in_blocks, precision=highest)
    lower_mask = jnp.arange(block)[:, None] >= jnp.arange(block)[None, :]
    differ = cumul[:, :, :, None, :] - cumul[:, :, None, :, :]
    decay = jnp.exp(jnp.where(lower_mask[None, None, :, :, None], differ, mask_fill))
    mixing = gram[..., None] * decay * step_blocks[:, :, None, :, :]
    inner = jnp.einsum("bcijh,bcjhp->bcihp", mixing, value_blocks, precision=highest)
    weight_end = jnp.exp(totals[:, :, None, :] - cumul) * step_blocks
    states = jnp.einsum(
        "bcjh,bcjn,bcjhp->bchnp", weight_end, in_blocks, value_blocks, precision=highest
    )

    def advance(carry, packed):
        total_now, state_now = packed
        return (jnp.exp(total_now)[..., None, None] * carry + state_now, carry)

    final_state, starts = lax.scan(
        advance, start, (jnp.moveaxis(totals, 1, 0), jnp.moveaxis(states, 1, 0))
    )
    starts = jnp.moveaxis(starts, 0, 1)
    carried = (
        jnp.einsum("bcin,bchnp->bcihp", out_blocks, starts, precision=highest)
        * jnp.exp(cumul)[..., None]
    )
    output = inner + carried + skip[:, None] * value_blocks
    offsets = jnp.cumsum(totals, axis=1) - totals
    cum_device = (cumul + offsets[:, :, None, :]).reshape(batch_count, row_count, head_count)
    decay_all = jnp.exp(jnp.sum(totals, axis=1))
    return (
        output.reshape(batch_count, row_count, head_count, head_width),
        final_state,
        cum_device,
        decay_all,
    )


def chain_join(earlier, later):
    return (earlier[0] * later[0], later[0][..., None, None] * earlier[1] + later[1])


def conv_inputs(conv_f, history, kernel, offset, step_raw, step_bias, decay_log):
    head_count = step_raw.shape[-1]
    batch_count, row_count, channels = conv_f.shape
    inner_width = channels - 2 * N
    activated = jax.nn.silu(causal_conv(conv_f, history, kernel, offset))
    values = activated[..., :inner_width].reshape(
        batch_count, row_count, head_count, inner_width // head_count
    )
    in_map = activated[..., inner_width : inner_width + N]
    out_map = activated[..., inner_width + N :]
    steps = jax.nn.softplus(step_raw + step_bias)
    rates = steps * -jnp.exp(decay_log)
    return (values, in_map, out_map, steps, rates)


def mamba_local(
    conv_f, history, step_raw, gate_z, start, kernel, offset, step_bias, decay_log, skip_gain
):
    values, in_map, out_map, steps, rates = conv_inputs(
        conv_f, history, kernel, offset, step_raw, step_bias, decay_log
    )
    result = state_blocks(values, in_map, out_map, steps, rates, skip_gain, start, SCAN_BLOCK)
    gated = result[0].reshape(gate_z.shape) * jax.nn.silu(gate_z)
    return (gated, result[1])


def block_scores(query_block, key_rows, query_pos, key_pos, length, attn_scale):
    scores = (
        jnp.einsum("qhd,kd->hqk", query_block, key_rows, preferred_element_type=jnp.float32)
        * attn_scale
    )
    allowed = (key_pos[None, :] <= query_pos[:, None]) & (key_pos[None, :] < length)
    return (scores, allowed)


def local(
    hidden,
    cotangent,
    lengths,
    norm1_gain,
    w_z,
    w_x,
    w_shared,
    w_dt,
    dt_bias,
    a_log,
    d_skip,
    conv_w,
    conv_b,
    gated_gain,
    w_out,
    w_q,
    w_o,
    norm2_gain,
    w_gate,
    w_up,
    w_down,
):
    slot_count, row_count, model_width = hidden.shape
    tp_count = lax.axis_size("tp")
    tp_rank = lax.axis_index("tp")
    ctx_count = lax.axis_size("ctx")
    ctx_rank = lax.axis_index("ctx")
    head_count = H // tp_count
    inner_width = head_count * P_SIZE
    query_count = NQ // tp_count
    kv_rank = tp_rank * query_count // (NQ // KV)
    total_rows = slot_count * row_count
    tail_rows = CONVW - 1
    attn_scale = HD ** (-0.5)
    layer_weights = (
        lax.all_gather(w_z, ("shard", "ctx"), axis=0, tiled=True),
        lax.all_gather(w_x, ("shard", "ctx"), axis=0, tiled=True),
        lax.all_gather(w_q, ("shard", "ctx"), axis=0, tiled=True),
        lax.all_gather(w_gate, ("shard", "ctx"), axis=0, tiled=True),
        lax.all_gather(w_up, ("shard", "ctx"), axis=0, tiled=True),
        lax.all_gather(w_out, ("shard", "ctx"), axis=1, tiled=True),
        lax.all_gather(w_o, ("shard", "ctx"), axis=1, tiled=True),
        lax.all_gather(w_down, ("shard", "ctx"), axis=1, tiled=True),
        lax.all_gather(norm1_gain, ("shard", "ctx"), axis=0, tiled=True),
        lax.all_gather(norm2_gain, ("shard", "ctx"), axis=0, tiled=True),
        lax.all_gather(w_shared, ("shard", "ctx"), axis=0, tiled=True),
        lax.all_gather(w_dt, ("shard", "ctx"), axis=0, tiled=True),
    )
    (
        full_z,
        full_x,
        full_q,
        full_gate,
        full_up,
        full_out,
        full_o,
        full_down,
        gain_one,
        gain_two,
        full_shared,
        full_dt,
    ) = layer_weights
    gain_one = gain_one.astype(jnp.float32)
    gain_two = gain_two.astype(jnp.float32)
    head_start = tp_rank * head_count
    chan_start = tp_rank * inner_width
    weight_map = full_shared[:, : 2 * N]
    key_cols = lax.dynamic_slice_in_dim(full_shared, 2 * N + kv_rank * HD, HD, 1)
    value_cols = lax.dynamic_slice_in_dim(full_shared, 2 * N + KV * HD + kv_rank * HD, HD, 1)
    weight_kv = jnp.concatenate([key_cols, value_cols], axis=1)
    weight_dt = lax.dynamic_slice_in_dim(full_dt, head_start, head_count, 1)
    step_bias = lax.dynamic_slice_in_dim(dt_bias.astype(jnp.float32), head_start, head_count, 0)
    decay_log = lax.dynamic_slice_in_dim(a_log.astype(jnp.float32), head_start, head_count, 0)
    skip_gain = lax.dynamic_slice_in_dim(d_skip.astype(jnp.float32), head_start, head_count, 0)
    kernel = jnp.concatenate(
        [lax.dynamic_slice_in_dim(conv_w, chan_start, inner_width, 1), conv_w[:, DI:]], axis=1
    ).astype(jnp.float32)
    offset = jnp.concatenate(
        [lax.dynamic_slice_in_dim(conv_b, chan_start, inner_width, 0), conv_b[DI:]], axis=0
    ).astype(jnp.float32)
    gain_gate = lax.dynamic_slice_in_dim(gated_gain.astype(jnp.float32), chan_start, inner_width, 0)
    inputs = hidden.astype(jnp.float32).reshape(total_rows, model_width)
    scale_one = lax.rsqrt(jnp.mean(inputs * inputs, -1, keepdims=True) + norm_epsilon)
    unit_one = inputs * scale_one
    normed = (unit_one * gain_one).astype(jnp.bfloat16)
    gate_z = matmul(normed, full_z)
    inner_x = matmul(normed, full_x)
    mapped = matmul(normed, weight_map)
    kv_rows = matmul(normed, weight_kv)
    step_raw = matmul(normed, weight_dt)
    query_rows = matmul(normed, full_q)
    conv_in = (
        jnp.concatenate([inner_x, mapped], axis=-1)
        .astype(jnp.bfloat16)
        .reshape(slot_count, row_count, inner_width + 2 * N)
    )
    pos_int = ctx_rank * row_count + jnp.arange(row_count, dtype=jnp.int32)
    cosine, sine = rotary_tables(pos_int.astype(jnp.float32), HD)
    keys_local = rotate(kv_rows[:, :HD].reshape(slot_count, row_count, HD), cosine, sine).astype(
        jnp.bfloat16
    )
    values_local = kv_rows[:, HD:].reshape(slot_count, row_count, HD).astype(jnp.bfloat16)
    conv_tail = conv_in[:, row_count - tail_rows :]
    keys_all, values_all, tails_all = (
        lax.all_gather(keys_local, "ctx", axis=1, tiled=True),
        lax.all_gather(values_local, "ctx", axis=1, tiled=True),
        lax.all_gather(conv_tail, "ctx", axis=1, tiled=True),
    )
    earlier_rank = jnp.maximum(ctx_rank - 1, 0)
    history = lax.dynamic_slice_in_dim(tails_all, earlier_rank * tail_rows, tail_rows, 1)
    history = jnp.where(ctx_rank > 0, history, jnp.zeros_like(history)).astype(jnp.float32)
    step_in = step_raw.reshape(slot_count, row_count, head_count)
    conv_f = conv_in.astype(jnp.float32)
    values, in_map, out_map, steps, rates = conv_inputs(
        conv_f, history, kernel, offset, step_in, step_bias, decay_log
    )
    zero_state = jnp.zeros((slot_count, head_count, N, P_SIZE), jnp.float32)
    local_out, local_state, cum_device, decay_all = state_blocks(
        values, in_map, out_map, steps, rates, skip_gain, zero_state, SCAN_BLOCK
    )
    carried_in = carried_in_2(
        (decay_all, local_state),
        "ctx",
        chain_join,
        (jnp.ones_like(decay_all), jnp.zeros_like(local_state)),
    )[1]
    ssd_out = (
        local_out
        + jnp.einsum("srn,shnp->srhp", out_map, carried_in, precision=highest)
        * jnp.exp(cum_device)[..., None]
    )
    gate_silu = jax.nn.silu(gate_z)
    gated = ssd_out.reshape(total_rows, inner_width) * gate_silu
    square_part = jnp.sum(gated * gated, -1)
    gated_low = (gated * gain_gate).astype(jnp.bfloat16)
    project_part = matmul(gated_low, full_out)
    queries = rotate(
        query_rows.reshape(slot_count, row_count, query_count, HD), cosine[:, None], sine[:, None]
    ).astype(jnp.bfloat16)
    block_count = row_count // QUERY_BLOCK
    key_pos = jnp.arange(ctx_count * row_count, dtype=jnp.int32)

    def block_inputs(flat_index):
        slot_index = flat_index // block_count
        block_index = flat_index % block_count
        query_block = lax.dynamic_slice(
            queries,
            (slot_index, block_index * QUERY_BLOCK, 0, 0),
            (1, QUERY_BLOCK, query_count, HD),
        )[0]
        key_rows = lax.dynamic_index_in_dim(keys_all, slot_index, 0, keepdims=False)
        value_rows = lax.dynamic_index_in_dim(values_all, slot_index, 0, keepdims=False)
        length = lax.dynamic_index_in_dim(lengths, slot_index, 0, keepdims=False)
        query_pos = (
            ctx_rank * row_count
            + block_index * QUERY_BLOCK
            + jnp.arange(QUERY_BLOCK, dtype=jnp.int32)
        )
        return (slot_index, block_index, query_block, key_rows, value_rows, length, query_pos)

    def forward_block(flat_index):
        slot_index, block_index, query_block, key_rows, value_rows, length, query_pos = (
            block_inputs(flat_index)
        )
        scores, allowed = block_scores(
            query_block, key_rows, query_pos, key_pos, length, attn_scale
        )
        masked = jnp.where(allowed[None], scores, mask_fill)
        peak = jnp.max(masked, axis=-1, keepdims=True)
        expo = jnp.exp(masked - peak)
        total = jnp.sum(expo, axis=-1, keepdims=True)
        probs = expo / total
        log_total = peak[..., 0] + jnp.log(total[..., 0])
        result = jnp.einsum(
            "hqk,kd->qhd",
            probs.astype(jnp.bfloat16),
            value_rows,
            preferred_element_type=jnp.float32,
        )
        return (result, log_total)

    flat_ids = jnp.arange(slot_count * block_count, dtype=jnp.int32)
    attended, log_totals = lax.map(forward_block, flat_ids)
    attended_low = attended.reshape(total_rows, query_count * HD).astype(jnp.bfloat16)
    attn_part = matmul(attended_low, full_o)
    project_all, attn_all, square_all = lax.psum((project_part, attn_part, square_part), "tp")
    mamba_scale = lax.rsqrt(square_all / DI + norm_epsilon)[:, None]
    resid = inputs + mamba_scale * project_all + attn_all
    scale_two = lax.rsqrt(jnp.mean(resid * resid, -1, keepdims=True) + norm_epsilon)
    unit_two = resid * scale_two
    normed_two = (unit_two * gain_two).astype(jnp.bfloat16)
    gate_h = matmul(normed_two, full_gate)
    up_h = matmul(normed_two, full_up)
    gate_sigmoid = jax.nn.sigmoid(gate_h)
    act_low = (gate_h * gate_sigmoid * up_h).astype(jnp.bfloat16)
    down_part = matmul(act_low, full_down).reshape(slot_count, row_count, model_width)
    mlp_share = lax.psum_scatter(
        down_part.astype(jnp.bfloat16), "tp", scatter_dimension=2, tiled=True
    ).astype(jnp.float32)
    share_width = model_width // tp_count
    resid_share = lax.dynamic_slice_in_dim(
        resid.reshape(slot_count, row_count, model_width), tp_rank * share_width, share_width, 2
    )
    output = (resid_share + mlp_share).astype(jnp.bfloat16)
    live = pos_int[None, :] < lengths[:, None]
    seed = jnp.where(live[..., None], cotangent.astype(jnp.float32), 0.0).reshape(
        total_rows, model_width
    )
    seed_low = seed.astype(jnp.bfloat16)
    first_tp = (tp_rank == 0).astype(jnp.float32)
    grad_act = matmul_nt(seed_low, full_down)
    grad_w_down = matmul_tn(act_low, seed_low)
    slope = gate_sigmoid * (1.0 + gate_h * (1.0 - gate_sigmoid))
    grad_gate = (grad_act * up_h * slope).astype(jnp.bfloat16)
    grad_up = (grad_act * gate_h * gate_sigmoid).astype(jnp.bfloat16)
    grad_two_part = matmul_nt(grad_gate, full_gate) + matmul_nt(grad_up, full_up)
    grad_w_gate = matmul_tn(normed_two, grad_gate)
    grad_w_up = matmul_tn(normed_two, grad_up)
    grad_normed_two = lax.psum(grad_two_part, "tp")
    weighted_two = grad_normed_two * gain_two
    grad_resid = seed + scale_two * (
        weighted_two - unit_two * jnp.mean(weighted_two * unit_two, -1, keepdims=True)
    )
    grad_gain_two = jnp.sum(grad_normed_two * unit_two, 0) * first_tp
    grad_scale = jnp.sum(grad_resid * project_all, -1, keepdims=True)
    grad_project = (mamba_scale * grad_resid).astype(jnp.bfloat16)
    grad_attn = grad_resid.astype(jnp.bfloat16)
    grad_w_out = matmul_tn(gated_low, grad_project)
    grad_gated_low = matmul_nt(grad_project, full_out)
    grad_gain_gate = jnp.sum(grad_gated_low * gated, 0)
    grad_gated = grad_gated_low * gain_gate - grad_scale * mamba_scale**3 * gated / DI
    grad_w_o = matmul_tn(attended_low, grad_attn)
    grad_attended = (
        matmul_nt(grad_attn, full_o)
        .astype(jnp.bfloat16)
        .reshape(slot_count, row_count, query_count, HD)
    )

    def backward_block(carry, flat_index):
        key_grad, value_grad = carry
        slot_index, block_index, query_block, key_rows, value_rows, length, query_pos = (
            block_inputs(flat_index)
        )
        grad_block = lax.dynamic_slice(
            grad_attended,
            (slot_index, block_index * QUERY_BLOCK, 0, 0),
            (1, QUERY_BLOCK, query_count, HD),
        )[0]
        log_total = lax.dynamic_index_in_dim(log_totals, flat_index, 0, keepdims=False)
        scores, allowed = block_scores(
            query_block, key_rows, query_pos, key_pos, length, attn_scale
        )
        probs = jnp.where(allowed[None], jnp.exp(scores - log_total[..., None]), 0.0)
        grad_probs = jnp.einsum(
            "qhd,kd->hqk", grad_block, value_rows, preferred_element_type=jnp.float32
        )
        row_dot = jnp.sum(probs * grad_probs, axis=-1, keepdims=True)
        grad_scores = (probs * (grad_probs - row_dot)).astype(jnp.bfloat16)
        grad_query = (
            jnp.einsum("hqk,kd->qhd", grad_scores, key_rows, preferred_element_type=jnp.float32)
            * attn_scale
        )
        grad_key = (
            jnp.einsum("hqk,qhd->kd", grad_scores, query_block, preferred_element_type=jnp.float32)
            * attn_scale
        )
        grad_value = jnp.einsum(
            "hqk,qhd->kd",
            probs.astype(jnp.bfloat16),
            grad_block,
            preferred_element_type=jnp.float32,
        )
        key_grad = lax.dynamic_update_index_in_dim(
            key_grad,
            lax.dynamic_index_in_dim(key_grad, slot_index, 0, keepdims=False) + grad_key,
            slot_index,
            0,
        )
        value_grad = lax.dynamic_update_index_in_dim(
            value_grad,
            lax.dynamic_index_in_dim(value_grad, slot_index, 0, keepdims=False) + grad_value,
            slot_index,
            0,
        )
        return ((key_grad, value_grad), grad_query)

    zero_keys = jnp.zeros((slot_count, ctx_count * row_count, HD), jnp.float32)
    (key_grad, value_grad), grad_queries = lax.scan(
        backward_block, (zero_keys, zero_keys), flat_ids
    )
    grad_queries = unrotate(
        grad_queries.reshape(slot_count, row_count, query_count, HD), cosine[:, None], sine[:, None]
    )
    grad_query_low = grad_queries.reshape(total_rows, query_count * HD).astype(jnp.bfloat16)
    grad_ssd = (grad_gated * gate_silu).reshape(slot_count, row_count, head_count, P_SIZE)
    back_state = jnp.einsum(
        "srh,srn,srhp->shnp", jnp.exp(cum_device), out_map, grad_ssd, precision=highest
    )
    later_grad = entering(
        (decay_all, back_state),
        "ctx",
        chain_join,
        (jnp.ones_like(decay_all), jnp.zeros_like(back_state)),
    )[1]
    gate_rows = gate_z.reshape(slot_count, row_count, inner_width)
    unused_out, pullback = jax.vjp(
        mamba_local,
        conv_f,
        history,
        step_in,
        gate_rows,
        carried_in,
        kernel,
        offset,
        step_bias,
        decay_log,
        skip_gain,
    )
    local_grads = pullback((grad_gated.reshape(slot_count, row_count, inner_width), later_grad))
    grad_conv, grad_history, grad_step, grad_z = (
        local_grads[0],
        local_grads[1],
        local_grads[2],
        local_grads[3],
    )
    grad_kernel, grad_offset, grad_bias, grad_decay, grad_skip = (
        local_grads[5],
        local_grads[6],
        local_grads[7],
        local_grads[8],
        local_grads[9],
    )
    channels = inner_width + 2 * N
    tail_grad = jnp.zeros((slot_count, tail_rows * ctx_count, channels), jnp.float32)
    tail_grad = lax.dynamic_update_slice_in_dim(
        tail_grad, jnp.where(ctx_rank > 0, grad_history, 0.0), earlier_rank * tail_rows, 1
    )
    key_own, value_own, tail_own = (
        lax.psum_scatter(
            key_grad.astype(jnp.bfloat16), "ctx", scatter_dimension=1, tiled=True
        ).astype(jnp.float32),
        lax.psum_scatter(
            value_grad.astype(jnp.bfloat16), "ctx", scatter_dimension=1, tiled=True
        ).astype(jnp.float32),
        lax.psum_scatter(
            tail_grad.astype(jnp.bfloat16), "ctx", scatter_dimension=1, tiled=True
        ).astype(jnp.float32),
    )
    grad_conv = jnp.concatenate(
        [grad_conv[:, : row_count - tail_rows], grad_conv[:, row_count - tail_rows :] + tail_own],
        axis=1,
    )
    grad_conv = grad_conv.reshape(total_rows, channels)
    grad_x_low = grad_conv[:, :inner_width].astype(jnp.bfloat16)
    grad_map = grad_conv[:, inner_width:]
    grad_z_low = grad_z.reshape(total_rows, inner_width).astype(jnp.bfloat16)
    grad_step_low = grad_step.reshape(total_rows, head_count).astype(jnp.bfloat16)
    grad_keys = unrotate(key_own, cosine, sine).reshape(total_rows, HD)
    grad_kv = jnp.concatenate([grad_keys, value_own.reshape(total_rows, HD)], axis=-1)
    grad_one_part = (
        matmul_nt(grad_z_low, full_z)
        + matmul_nt(grad_x_low, full_x)
        + matmul_nt(grad_step_low, weight_dt)
        + matmul_nt(grad_query_low, full_q)
        + precise_nt(grad_map, weight_map.astype(jnp.float32))
        + precise_nt(grad_kv, weight_kv.astype(jnp.float32))
    )
    normed_wide = normed.astype(jnp.float32)
    grad_w_z = matmul_tn(normed, grad_z_low)
    grad_w_x = matmul_tn(normed, grad_x_low)
    grad_w_q = matmul_tn(normed, grad_query_low)
    grad_dt_cols = matmul_tn(normed, grad_step_low)
    grad_map_w = precise_tn(normed_wide, grad_map)
    grad_kv_w = precise_tn(normed_wide, grad_kv)
    grad_shared = jnp.zeros((model_width, full_shared.shape[1]), jnp.float32)
    grad_shared = lax.dynamic_update_slice_in_dim(grad_shared, grad_map_w, 0, 1)
    grad_shared = lax.dynamic_update_slice_in_dim(
        grad_shared, grad_kv_w[:, :HD], 2 * N + kv_rank * HD, 1
    )
    grad_shared = lax.dynamic_update_slice_in_dim(
        grad_shared, grad_kv_w[:, HD:], 2 * N + KV * HD + kv_rank * HD, 1
    )
    grad_w_dt = lax.dynamic_update_slice_in_dim(
        jnp.zeros((model_width, H), jnp.float32), grad_dt_cols, head_start, 1
    )
    grad_normed = lax.psum(grad_one_part.astype(jnp.bfloat16), "tp").astype(jnp.float32)
    weighted_one = grad_normed * gain_one
    grad_hidden = grad_resid + scale_one * (
        weighted_one - unit_one * jnp.mean(weighted_one * unit_one, -1, keepdims=True)
    )
    grad_gain_one = jnp.sum(grad_normed * unit_one, 0) * first_tp
    share_one, share_two, share_shared, share_dt = (
        lax.psum_scatter(grad_gain_one, ("shard", "ctx", "tp"), scatter_dimension=0, tiled=True),
        lax.psum_scatter(grad_gain_two, ("shard", "ctx", "tp"), scatter_dimension=0, tiled=True),
        lax.psum_scatter(grad_shared, ("shard", "ctx", "tp"), scatter_dimension=0, tiled=True),
        lax.psum_scatter(grad_w_dt, ("shard", "ctx", "tp"), scatter_dimension=0, tiled=True),
    )
    layer_grads = (
        lax.psum_scatter(grad_w_z, ("shard", "ctx"), scatter_dimension=0, tiled=True),
        lax.psum_scatter(grad_w_x, ("shard", "ctx"), scatter_dimension=0, tiled=True),
        lax.psum_scatter(grad_w_q, ("shard", "ctx"), scatter_dimension=0, tiled=True),
        lax.psum_scatter(grad_w_gate, ("shard", "ctx"), scatter_dimension=0, tiled=True),
        lax.psum_scatter(grad_w_up, ("shard", "ctx"), scatter_dimension=0, tiled=True),
        lax.psum_scatter(grad_w_out, ("shard", "ctx"), scatter_dimension=1, tiled=True),
        lax.psum_scatter(grad_w_o, ("shard", "ctx"), scatter_dimension=1, tiled=True),
        lax.psum_scatter(grad_w_down, ("shard", "ctx"), scatter_dimension=1, tiled=True),
    )
    bias_full = lax.dynamic_update_slice_in_dim(
        jnp.zeros((H,), jnp.float32), grad_bias, head_start, 0
    )
    decay_full = lax.dynamic_update_slice_in_dim(
        jnp.zeros((H,), jnp.float32), grad_decay, head_start, 0
    )
    skip_full = lax.dynamic_update_slice_in_dim(
        jnp.zeros((H,), jnp.float32), grad_skip, head_start, 0
    )
    kernel_full = jnp.zeros((CONVW, DI + 2 * N), jnp.float32)
    kernel_full = lax.dynamic_update_slice_in_dim(
        kernel_full, grad_kernel[:, :inner_width], chan_start, 1
    )
    kernel_full = lax.dynamic_update_slice_in_dim(kernel_full, grad_kernel[:, inner_width:], DI, 1)
    offset_full = jnp.zeros((DI + 2 * N,), jnp.float32)
    offset_full = lax.dynamic_update_slice_in_dim(
        offset_full, grad_offset[:inner_width], chan_start, 0
    )
    offset_full = lax.dynamic_update_slice_in_dim(offset_full, grad_offset[inner_width:], DI, 0)
    gate_full = lax.dynamic_update_slice_in_dim(
        jnp.zeros((DI,), jnp.float32), grad_gain_gate, chan_start, 0
    )
    small_all = lax.psum(
        (bias_full, decay_full, skip_full, kernel_full, offset_full, gate_full),
        ("shard", "ctx", "tp"),
    )
    return (
        output,
        grad_hidden.reshape(slot_count, row_count, model_width),
        share_one,
        layer_grads[0],
        layer_grads[1],
        share_shared,
        share_dt,
        small_all[0],
        small_all[1],
        small_all[2],
        small_all[3],
        small_all[4],
        small_all[5],
        layer_grads[5],
        layer_grads[2],
        layer_grads[6],
        share_two,
        layer_grads[3],
        layer_grads[4],
        layer_grads[7],
    )


def solution(mesh):
    placed = (
        P("shard", "ctx", None),
        P("shard", "ctx", None),
        P("shard"),
        P(("shard", "ctx")),
        P(("shard", "ctx"), "tp"),
        P(("shard", "ctx"), "tp"),
        P(("shard", "ctx"), None),
        P(("shard", "ctx"), None),
        P(),
        P(),
        P(),
        P(),
        P(),
        P(),
        P("tp", ("shard", "ctx")),
        P(("shard", "ctx"), "tp"),
        P("tp", ("shard", "ctx")),
        P(("shard", "ctx")),
        P(("shard", "ctx"), "tp"),
        P(("shard", "ctx"), "tp"),
        P("tp", ("shard", "ctx")),
    )
    return jax.shard_map(
        local,
        mesh=mesh,
        in_specs=placed,
        out_specs=(
            P("shard", "ctx", "tp"),
            P("shard", "ctx", None),
            P(("shard", "ctx", "tp")),
            P(("shard", "ctx"), "tp"),
            P(("shard", "ctx"), "tp"),
            P(("shard", "ctx", "tp"), None),
            P(("shard", "ctx", "tp"), None),
            P(),
            P(),
            P(),
            P(),
            P(),
            P(),
            P("tp", ("shard", "ctx")),
            P(("shard", "ctx"), "tp"),
            P("tp", ("shard", "ctx")),
            P(("shard", "ctx", "tp")),
            P(("shard", "ctx"), "tp"),
            P(("shard", "ctx"), "tp"),
            P("tp", ("shard", "ctx")),
        ),
        check_vma=False,
    )
```

profile of v0, /device:TPU:0, one launch (start us, length us, event | category | flops | bytes accessed | tf_op | source)
XLA Modules:
  0.0 1513.7 jit_solution(7358748829974008269)
XLA Ops:
  12.4 13.5 all-gather.6
  28.0 12.9 all_gather.69
  43.0 7.2 reduce-window.14
  52.0 14.2 all_gather.75
  66.2 14.1 all_gather.78
  94.2 16.4 %all_gather.66 = bf16[1024,384]{1,0:T(8,128)(2,1)S(1)} all-gather(bf16[128,384]{1,0:T(8,128)(2,1)} %param.40), channel_id=1, replica_groups=mesh['shard'=4,'ctx'=2,'tp'=4] {'shard','ctx'}, dimensions={0}, use_global_device_ids=true | all-gather | bytes 884736 | tf_op jit(solution)/shard_map/all_gather | solution.py:252
  112.6 17.1 %all_gather.73 = bf16[1024,384]{1,0:T(8,128)(2,1)} all-gather(bf16[128,384]{1,0:T(8,128)(2,1)S(1)} %copy-done.107), channel_id=1, replica_groups=mesh['shard'=4,'ctx'=2,'tp'=4] {'shard','ctx'}, dimensions={0}, use_global_device_ids=true | all-gather | bytes 884736 | tf_op jit(solution)/shard_map/all_gather | solution.py:251
  129.6 16.2 %all_gather.74 = bf16[384,1024]{1,0:T(8,128)(2,1)} all-gather(bf16[384,128]{1,0:T(8,128)(2,1)S(1)} %copy-done.108), channel_id=1, replica_groups=mesh['shard'=4,'ctx'=2,'tp'=4] {'shard','ctx'}, dimensions={1}, use_global_device_ids=true | all-gather | bytes 884736 | tf_op jit(solution)/shard_map/all_gather | solution.py:256
  155.0 9.1 fusion.107
  180.2 25.4 %while.113 = (s32[]{:T(128)}, bf16[2,512,2,64]{1,3,2,0:T(8,128)(2,1)}, f32[2,2,512]{2,1,0:T(2,128)S(1)}, s32[2]{0:T(128)S(1)}, s32[]{:T(128)}, /*index=5*/s32[1]...) while((s32[]{:T(128)}, ...), condition=%wide.region_15.16_spmd.clone.clone, body=%wide.region_12.15_spmd.clone.clone.sunk | while | flops 564135424 | bytes 32416140 | solution.py:398
  225.9 7.6 while.115
  243.0 10.0 while.111
  264.8 8.5 fusion.120
  292.1 8.7 all-gather.7
  300.8 10.1 psum.77
  310.9 150.2 %all-reduce.28.cloned.1.call-done = (f32[1024,1024]{1,0:T(8,128)}, f32[1024,1024]{1,0:T(8,128)}) async-done(((f32[1024,1024]{1,0:T(8,128)}, f32[1024,1024]{1,0:T(8,128)}), (f32[1024,1024]{1,0:T(8,128)}, f32[1024,1024]{1,0:T(8,128)})) %all-reduce.28.cloned.1.call-update) | async-done | bytes 8388624 | tf_op jit(solution)/shard_map/psum | solution.py:401
  468.1 17.6 %all-gather.17.cloned.1.call-done = bf16[1024,512]{1,0:T(8,128)(2,1)} async-done(((bf16[128,512]{1,0:T(8,128)(2,1)}), bf16[1024,512]{1,0:T(8,128)(2,1)}) %all-gather.17.cloned.1.call-update) | async-done | bytes 1048592 | tf_op jit(solution)/shard_map/all_gather | solution.py:255
  489.4 19.5 %all-gather.15.cloned.1.call-done = bf16[1024,512]{1,0:T(8,128)(2,1)} async-done(((bf16[128,512]{1,0:T(8,128)(2,1)}), bf16[1024,512]{1,0:T(8,128)(2,1)}) %all-gather.15.cloned.1.call-update) | async-done | bytes 1048592 | tf_op jit(solution)/shard_map/all_gather | solution.py:254
  512.8 21.3 %all-gather.19.cloned.1.call-done = bf16[512,1024]{1,0:T(8,128)(2,1)} async-done(((bf16[512,128]{1,0:T(8,128)(2,1)}), bf16[512,1024]{1,0:T(8,128)(2,1)}) %all-gather.19.cloned.1.call-update) | async-done | bytes 1048592 | tf_op jit(solution)/shard_map/all_gather | solution.py:258
  534.1 6.3 multiply_convert_fusion.2
  545.7 102.6 %all-reduce.24.cloned.1.call-done = f32[1024,1024]{1,0:T(8,128)} async-done(((f32[1024,1024]{1,0:T(8,128)}), f32[1024,1024]{1,0:T(8,128)}) %all-reduce.24.cloned.1.call-update) | async-done | bytes 4194320 | tf_op jit(solution)/shard_map/psum | solution.py:434
  648.3 4.7 multiply_reduce_fusion.1
  660.4 38.6 %while.114 = (s32[]{:T(128)}, f32[1,2048,64]{1,2,0:T(8,128)S(1)}, f32[1,2048,64]{1,2,0:T(8,128)S(1)}, f32[2,512,2,64]{1,0,3,2:T(2,128)S(1)}, s32[2]{0:T(128)S(1)...) while((s32[]{:T(128)}, f32[1,2048,64]{1,2,0:T(8,128)S(1)}, ...), condition=%wide.region_40.41_spmd.clone.clone, body=%wide.region_38.40_spmd.clone.clone.sunk | while | flops 1376192000 | bytes 71864720 | solution.py:503
  711.7 6.6 fusion.112
  726.8 6.0 fusion.154
  743.9 13.7 while.112
  762.0 11.8 fusion.90
  773.8 6.8 bitcast_add_fusion.5
  800.1 30.2 %reduce-window.16 = f32[1,4,6,2,128]{4,3,2,1,0:T(2,128)S(1)} reduce-window(f32[1,4,6,2,128]{4,3,2,1,0:T(2,128)S(1)} %copy.635, f32[]{:T(128)} %constant.396.clone.1), window={size=1x1x1x1x128 pad=0_0x0_0x0_0x0_0x0_127}, to_apply=%region_36.37 | reduce-window | flops 780288 | bytes 49156 | tf_op jit(solution)/shard_map/reduce-window.2
  831.5 10.9 multiply_reduce_fusion.7
  855.4 6.5 pad_add_fusion
  892.5 10.5 add_convert_fusion
  903.1 4.6 fusion.182
  907.8 4.6 fusion.284
  920.7 4.7 fusion.216
  930.3 4.9 fusion.257
  962.5 53.9 %reduce-scatter.40.cloned.1.call-done = f32[32,24]{1,0:T(8,128)} async-done(((f32[1024,24]{1,0:T(8,128)}), f32[32,24]{1,0:T(8,128)}) %reduce-scatter.40.cloned.1.call-update) | async-done | bytes 3088
  1017.8 67.4 %all-reduce.26.cloned.1.call-done = bf16[1024,1024]{1,0:T(8,128)(2,1)} async-done(((bf16[1024,1024]{1,0:T(8,128)(2,1)}), bf16[1024,1024]{1,0:T(8,128)(2,1)}) %all-reduce.26.cloned.1.call-update) | async-done | bytes 2097168 | tf_op jit(solution)/shard_map/psum | solution.py:601
  1088.3 41.4 %all-reduce.18 = (f32[1024]{0:T(1024)S(1)}, f32[24]{0:T(128)}, f32[24]{0:T(128)}, f32[24]{0:T(128)}, f32[4,1792]{1,0:T(4,128)}, /*index=5*/f32[1792]{0:T(1024)}, f32[1536]{0:T(1024)}, f32[1024]{0:T(1024)S(1)}) all-reduce(f32[1024]{0:T(1024)S(1)} %broadcast_multiply_fusion.8, ...), channel_id=12, replica_groups=mesh['shard'=4,'ctx'=2,'tp'=4] {'shard','ctx','tp'}, use_global_device_ids=true, to_apply=%region_46.47.clone | all-reduce | flops 12616 | bytes 100928
  1130.8 5.0 fusion.81
  1135.8 26.1 %reduce-scatter.34.cloned.1.call-done = f32[128,512]{1,0:T(8,128)} async-done(((f32[1024,512]{1,0:T(8,128)}), f32[128,512]{1,0:T(8,128)}) %reduce-scatter.34.cloned.1.call-update) | async-done | bytes 262160 | tf_op jit(solution)/shard_map/reduce_scatter | solution.py:617
  1161.8 37.2 %reduce-scatter.36.cloned.1.call-done = f32[128,512]{1,0:T(8,128)} async-done(((f32[1024,512]{1,0:T(8,128)}), f32[128,512]{1,0:T(8,128)}) %reduce-scatter.36.cloned.1.call-update) | async-done | bytes 262160 | tf_op jit(solution)/shard_map/reduce_scatter | solution.py:618
  1199.0 32.4 %reduce-scatter.32.cloned.1.call-done = f32[128,128]{1,0:T(8,128)} async-done(((f32[128,1024]{1,0:T(8,128)}), f32[128,128]{1,0:T(8,128)}) %reduce-scatter.32.cloned.1.call-update) | async-done | bytes 65552 | tf_op jit(solution)/shard_map/reduce_scatter | solution.py:620
  1231.4 31.8 %reduce-scatter.30.cloned.1.call-done = f32[128,128]{1,0:T(8,128)} async-done(((f32[1024,128]{1,0:T(8,128)}), f32[128,128]{1,0:T(8,128)}) %reduce-scatter.30.cloned.1.call-update) | async-done | bytes 65552 | tf_op jit(solution)/shard_map/reduce_scatter | solution.py:616
  1263.2 35.3 %reduce-scatter.28.cloned.1.call-done = f32[384,128]{1,0:T(8,128)} async-done(((f32[384,1024]{1,0:T(8,128)}), f32[384,128]{1,0:T(8,128)}) %reduce-scatter.28.cloned.1.call-update) | async-done | bytes 196624 | tf_op jit(solution)/shard_map/reduce_scatter | solution.py:619
  1298.5 35.0 %reduce-scatter.22.cloned.1.call-done = f32[128,384]{1,0:T(8,128)} async-done(((f32[1024,384]{1,0:T(8,128)}), f32[128,384]{1,0:T(8,128)}) %reduce-scatter.22.cloned.1.call-update) | async-done | bytes 196624 | tf_op jit(solution)/shard_map/reduce_scatter | solution.py:614
  1333.5 35.3 %reduce-scatter.24.cloned.1.call-done = f32[128,384]{1,0:T(8,128)} async-done(((f32[1024,384]{1,0:T(8,128)}), f32[128,384]{1,0:T(8,128)}) %reduce-scatter.24.cloned.1.call-update) | async-done | bytes 196624 | tf_op jit(solution)/shard_map/reduce_scatter | solution.py:615
  1368.8 137.5 %reduce-scatter.26.cloned.1.call-done = f32[32,512]{1,0:T(8,128)} async-done(((f32[1024,512]{1,0:T(8,128)}), f32[32,512]{1,0:T(8,128)}) %reduce-scatter.26.cloned.1.call-update) | async-done | bytes 65552 | tf_op jit(solution)/shard_map/reduce_scatter | solution.py:610
  (742 shorter events, 370.4 us)
Async XLA Ops:
  7.2 138.7 %all-gather.13.cloned.1.call-start = ((), (), s32[]{:S(2)}) async-start(), calls=%async_computation.13 | async-start | bytes 1179648 | tf_op jit(solution)/shard_map/all_gather | solution.py:261
  7.9 453.2 %all-reduce.28.cloned.1.call-start = ((), (), s32[]{:S(2)}) async-start(), calls=%async_computation.32 | async-start | bytes 16777216 | tf_op jit(solution)/shard_map/psum | solution.py:401
  11.4 29.5 %copy-start.154 = (f32[24]{0:T(128)}, f32[24]{0:T(128)S(1)}, u32[]{:S(2)}) copy-start(f32[24]{0:T(128)S(1)} %convert_element_type.276) | copy-start | bytes 292
  11.4 29.5 %copy-start.5 = (bf16[1,1024,1024]{2,1,0:T(8,128)(2,1)S(1)}, bf16[1,1024,1024]{2,1,0:T(8,128)(2,1)}, u32[]{:S(2)}) copy-start(bf16[1,1024,1024]{2,1,0:T(8,128)(2,1)} %param.35) | copy-start | bytes 6291460
  11.5 30.1 %copy-start.147 = (f32[6]{0:T(128)}, f32[6]{0:T(128)S(1)}, u32[]{:S(2)}) copy-start(f32[6]{0:T(128)S(1)} %fusion.244) | copy-start | bytes 76
  25.9 15.7 %copy-start.109 = (f32[8,1,128]{2,1,0:T(1,128)}, f32[8,1,128]{2,1,0:T(1,128)S(1)}, u32[]{:S(2)}) copy-start(f32[8,1,128]{2,1,0:T(1,128)S(1)} %convert_element_type.325) | copy-start | bytes 12292
  28.0 14.9 copy-start.111
  41.0 25.2 %copy-start.126 = (bf16[128,128]{1,0:T(8,128)(2,1)S(1)}, bf16[128,128]{1,0:T(8,128)(2,1)}, u32[]{:S(2)}) copy-start(bf16[128,128]{1,0:T(8,128)(2,1)} %param.51) | copy-start | bytes 98308
  41.6 240.1 %copy-start.3 = (bf16[1024,1024]{1,0:T(8,128)(2,1)}, bf16[1024,1024]{1,0:T(8,128)(2,1)S(1)}, u32[]{:S(2)}) copy-start(bf16[1024,1024]{1,0:T(8,128)(2,1)S(1)} %fusion.82) | copy-start | bytes 6291460
  42.9 45.1 %copy-start.98 = (f32[1024,6]{0,1:T(8,128)}, f32[1024,6]{0,1:T(8,128)S(1)}, u32[]{:S(2)}) copy-start(f32[1024,6]{0,1:T(8,128)S(1)} %get-tuple-element.1367) | copy-start | bytes 73732
  42.9 39.0 %copy-start.151 = (u32[32]{0:T(128)S(1)}, u32[32]{0:T(128)}, u32[]{:S(2)}) copy-start(u32[32]{0:T(128)} %constant.450) | copy-start | bytes 388
  42.9 45.2 %copy-start.158 = (bf16[24]{0:T(256)(128)(2,1)S(1)}, bf16[24]{0:T(256)(128)(2,1)}, u32[]{:S(2)}) copy-start(bf16[24]{0:T(256)(128)(2,1)} %param.45) | copy-start | bytes 148
  50.8 37.3 %copy-start.89 = (f32[1,4,256,6]{2,1,3,0:T(4,128)}, f32[1,4,256,6]{2,1,3,0:T(4,128)S(1)}, u32[]{:S(2)}) copy-start(f32[1,4,256,6]{2,1,3,0:T(4,128)S(1)} %get-tuple-element.1324) | copy-start | bytes 73732
  52.0 102.9 %copy-start.117 = (f32[640]{0:T(1024)}, f32[640]{0:T(1024)S(1)}, u32[]{:S(2)}) copy-start(f32[640]{0:T(1024)S(1)} %get-tuple-element.1196) | copy-start | bytes 7684
  66.2 21.8 %copy-start.70 = (bf16[1024,128]{1,0:T(8,128)(2,1)}, bf16[1024,128]{1,0:T(8,128)(2,1)S(1)}, u32[]{:S(2)}) copy-start(bf16[1024,128]{1,0:T(8,128)(2,1)S(1)} %all_gather.75) | copy-start | bytes 786436
  81.9 30.7 %copy-start.45 = (f32[1024,128]{0,1:T(8,128)}, f32[1024,128]{0,1:T(8,128)S(1)}, u32[]{:S(2)}) copy-start(f32[1024,128]{0,1:T(8,128)S(1)} %fusion.276) | copy-start | bytes 1572868
  110.6 19.1 %copy-start.53 = (bf16[1024,384]{1,0:T(8,128)(2,1)}, bf16[1024,384]{1,0:T(8,128)(2,1)S(1)}, u32[]{:S(2)}) copy-start(bf16[1024,384]{1,0:T(8,128)(2,1)S(1)} %all_gather.66) | copy-start | bytes 2359300
  110.6 19.1 %copy-start.108 = (bf16[384,128]{1,0:T(8,128)(2,1)S(1)}, bf16[384,128]{1,0:T(8,128)(2,1)}, u32[]{:S(2)}) copy-start(bf16[384,128]{1,0:T(8,128)(2,1)} %param.49) | copy-start | bytes 294916
  289.5 171.7 %copy-start.6 = (bf16[1,1024,1024]{2,1,0:T(8,128)(2,1)S(1)}, bf16[1,1024,1024]{2,1,0:T(8,128)(2,1)}, u32[]{:S(2)}) copy-start(bf16[1,1024,1024]{2,1,0:T(8,128)(2,1)} %param.35) | copy-start | bytes 6291460
  289.5 196.1 %all-gather.17.cloned.1.call-start = ((), (), s32[]{:S(2)}) async-start(), calls=%async_computation.15 | async-start | bytes 1179648 | tf_op jit(solution)/shard_map/all_gather | solution.py:255
  290.2 218.7 %all-gather.15.cloned.1.call-start = ((), (), s32[]{:S(2)}) async-start(), calls=%async_computation.14 | async-start | bytes 1179648 | tf_op jit(solution)/shard_map/all_gather | solution.py:254
  290.8 243.3 %all-gather.19.cloned.1.call-start = ((), (), s32[]{:S(2)}) async-start(), calls=%async_computation.16 | async-start | bytes 1179648 | tf_op jit(solution)/shard_map/all_gather | solution.py:258
  291.4 356.9 %all-reduce.24.cloned.1.call-start = ((), (), s32[]{:S(2)}) async-start(), calls=%async_computation.18 | async-start | bytes 8388608 | tf_op jit(solution)/shard_map/psum | solution.py:434
  292.1 361.5 %copy-start.144 = (pred[1024]{0:T(1024)(128)(4,1)}, pred[1024]{0:T(1024)(128)(4,1)S(1)}, u32[]{:S(2)}) copy-start(pred[1024]{0:T(1024)(128)(4,1)S(1)} %fusion.240) | copy-start | bytes 3076
  468.0 40.9 %copy-start.73 = (bf16[1024,1024]{1,0:T(8,128)(2,1)}, bf16[1024,1024]{1,0:T(8,128)(2,1)S(1)}, u32[]{:S(2)}) copy-start(bf16[1024,1024]{1,0:T(8,128)(2,1)S(1)} %multiply_convert_fusion.1) | copy-start | bytes 6291460
  512.8 27.6 %copy-start.157 = (bf16[1024,512]{1,0:T(8,128)(2,1)S(1)}, bf16[1024,512]{1,0:T(8,128)(2,1)}, u32[]{:S(2)}) copy-start(bf16[1024,512]{1,0:T(8,128)(2,1)} %all-gather.15.cloned.1.call-done) | copy-start | bytes 3145732
  545.7 336.8 %reduce-scatter.18.cloned.1.call-start = ((), (), s32[]{:S(2)}) async-start(), calls=%async_computation.19 | async-start | bytes 393216 | tf_op jit(solution)/shard_map/reduce_scatter | solution.py:554
  660.3 40.7 %copy-start.160 = (f32[12]{0:T(128)S(1)}, f32[12]{0:T(128)}, u32[]{:S(2)}) copy-start(f32[12]{0:T(128)} %copy-done.159) | copy-start | bytes 148
  660.3 43.2 %copy-start.100 = (f32[1024,6]{0,1:T(8,128)S(1)}, f32[1024,6]{0,1:T(8,128)}, u32[]{:S(2)}) copy-start(f32[1024,6]{0,1:T(8,128)} %copy-done.98) | copy-start | bytes 73732
  699.8 185.8 %reduce-scatter.20.cloned.1.call-start = ((), (), s32[]{:S(2)}) async-start(), calls=%async_computation.20 | async-start | bytes 393216 | tf_op jit(solution)/shard_map/reduce_scatter | solution.py:557
  701.0 259.2 %reduce-scatter.16.cloned.1.call-start = ((), (), s32[]{:S(2)}) async-start(), calls=%async_computation.17 | async-start | bytes 2621440 | tf_op jit(solution)/shard_map/reduce_scatter | solution.py:412
  711.7 304.8 %reduce-scatter.40.cloned.1.call-start = ((), (), s32[]{:S(2)}) async-start(), calls=%async_computation.31 | async-start | bytes 540672
  797.5 33.2 %copy-start.106 = (f32[1024,6]{0,1:T(8,128)S(1)}, f32[1024,6]{0,1:T(8,128)}, u32[]{:S(2)}) copy-start(f32[1024,6]{0,1:T(8,128)} %get-tuple-element.1378) | copy-start | bytes 73732
  797.5 33.2 %copy-start.148 = (f32[6]{0:T(128)S(1)}, f32[6]{0:T(128)}, u32[]{:S(2)}) copy-start(f32[6]{0:T(128)} %copy-done.147) | copy-start | bytes 76
  797.5 33.9 %copy-start.35 = (bf16[1,1024,384]{1,2,0:T(8,128)(2,1)S(1)}, bf16[1,1024,384]{1,2,0:T(8,128)(2,1)}, u32[]{:S(2)}) copy-start(bf16[1,1024,384]{1,2,0:T(8,128)(2,1)} %fusion.146) | copy-start | bytes 2359300
  797.5 33.9 %copy-start.41 = (bf16[1,1024,256]{1,2,0:T(8,128)(2,1)S(1)}, bf16[1,1024,256]{1,2,0:T(8,128)(2,1)}, u32[]{:S(2)}) copy-start(bf16[1,1024,256]{1,2,0:T(8,128)(2,1)} %copy-done.40) | copy-start | bytes 1572868
  882.4 202.8 %all-reduce.26.cloned.1.call-start = ((), (), s32[]{:S(2)}) async-start(), calls=%async_computation.21 | async-start | bytes 4194304 | tf_op jit(solution)/shard_map/psum | solution.py:601
  903.1 232.7 %reduce-scatter.38.cloned.1.call-start = ((), (), s32[]{:S(2)}) async-start(), calls=%async_computation.30 | async-start | bytes 2359296 | tf_op jit(solution)/shard_map/reduce_scatter | solution.py:621
  907.7 254.1 %reduce-scatter.34.cloned.1.call-start = ((), (), s32[]{:S(2)}) async-start(), calls=%async_computation.28 | async-start | bytes 2359296 | tf_op jit(solution)/shard_map/reduce_scatter | solution.py:617
  912.4 286.6 %reduce-scatter.36.cloned.1.call-start = ((), (), s32[]{:S(2)}) async-start(), calls=%async_computation.29 | async-start | bytes 2359296 | tf_op jit(solution)/shard_map/reduce_scatter | solution.py:618
  916.9 314.5 %reduce-scatter.32.cloned.1.call-start = ((), (), s32[]{:S(2)}) async-start(), calls=%async_computation.27 | async-start | bytes 589824 | tf_op jit(solution)/shard_map/reduce_scatter | solution.py:620
  920.5 342.7 %reduce-scatter.30.cloned.1.call-start = ((), (), s32[]{:S(2)}) async-start(), calls=%async_computation.26 | async-start | bytes 589824 | tf_op jit(solution)/shard_map/reduce_scatter | solution.py:616
  930.2 368.3 %reduce-scatter.28.cloned.1.call-start = ((), (), s32[]{:S(2)}) async-start(), calls=%async_computation.25 | async-start | bytes 1769472 | tf_op jit(solution)/shard_map/reduce_scatter | solution.py:619
  935.2 398.3 %reduce-scatter.22.cloned.1.call-start = ((), (), s32[]{:S(2)}) async-start(), calls=%async_computation.22 | async-start | bytes 1769472 | tf_op jit(solution)/shard_map/reduce_scatter | solution.py:614
  939.7 429.1 %reduce-scatter.24.cloned.1.call-start = ((), (), s32[]{:S(2)}) async-start(), calls=%async_computation.23 | async-start | bytes 1769472 | tf_op jit(solution)/shard_map/reduce_scatter | solution.py:615
  943.8 562.6 %reduce-scatter.26.cloned.1.call-start = ((), (), s32[]{:S(2)}) async-start(), calls=%async_computation.24 | async-start | bytes 2162688 | tf_op jit(solution)/shard_map/reduce_scatter | solution.py:610
  955.5 129.7 %copy-start.8 = (bf16[1,1024,1024]{2,1,0:T(8,128)(2,1)S(1)}, bf16[1,1024,1024]{2,1,0:T(8,128)(2,1)}, u32[]{:S(2)}) copy-start(bf16[1,1024,1024]{2,1,0:T(8,128)(2,1)} %param.35) | copy-start | bytes 6291460
  962.5 125.7 %copy-start.141 = (f32[1024]{0:T(1024)S(1)}, f32[1024]{0:T(1024)}, u32[]{:S(2)}) copy-start(f32[1024]{0:T(1024)} %get-tuple-element.1381) | copy-start | bytes 12292
  (141 other events, 666.7 us)
Sparse Core Ops, SparseCore 0:
  9.6 24.8 all-gather.12
  289.6 171.4 all-reduce.27
  462.8 22.7 all-gather.16
  487.2 21.7 all-gather.14
  510.4 23.5 all-gather.18
  545.8 102.4 all-reduce.23
  699.9 7.6 reduce-scatter.17
  710.5 8.8 reduce-scatter.19
  722.3 36.3 reduce-scatter.15
  882.5 133.8 reduce-scatter.39
  1019.6 65.6 all-reduce.25
  1088.1 35.8 reduce-scatter.37
  1127.0 34.8 reduce-scatter.33
  1164.7 34.2 reduce-scatter.35
  1201.8 29.5 reduce-scatter.31
  1234.1 29.1 reduce-scatter.29
  1266.1 32.4 reduce-scatter.27
  1301.4 32.0 reduce-scatter.21
  1336.5 32.3 reduce-scatter.23
  1371.6 134.7 reduce-scatter.25
where the time goes:
time: 1520 us; the launch traced here: 1510 us
  waiting for transfers between devices  806 us (53%)
  matrix products  203 us (13%)
  blocking collectives  184 us (12%)
  other arithmetic  157 us (10%)
  local copies, waits for them, and re-layouts  132 us (9%)
  between operations  18.9 us (1%)
    psum x1, waiting for transfers between devices, local(): lax.psum((project_part, attn_part, square_part), 'tp')  150 us
    reduce_scatter x1, waiting for transfers between devices, local(): lax.psum_scatter(grad_shared, ('shard', 'ctx', 'tp'), scatter_dimension=0...  138 us
    psum x1, waiting for transfers between devices, local(): grad_normed_two = lax.psum(grad_two_part, 'tp')  103 us
    psum x1, waiting for transfers between devices, local(): lax.psum(grad_one_part.astype(jnp.bfloat16), 'tp').astype(jnp.float32)  67.4 us
    unnamed x21, waiting for transfers between devices  56.6 us
    unnamed x4, blocking collectives  49.6 us
    another operation x9, other arithmetic  37.6 us
    reduce_scatter x1, waiting for transfers between devices, local(): lax.psum_scatter(grad_w_up, ('shard', 'ctx'), scatter_dimension=0, tiled=...  37.2 us
  transfers between devices with their start and end apart: 20, of which 15 were waited for; matrix products, arithmetic and copies ran while one was open for 19% of the time, Pallas kernels for 0%

commit v1 on v0

v1 whole, which is shorter than its diff:
```python
import functools

import jax
import jax.numpy as jnp
from jax import lax
from jax.experimental import pallas as pl
from jax.experimental.pallas import tpu as pltpu
from jax.sharding import PartitionSpec as P

H = 24
P_SIZE = 64
N = 128
NQ = 8
KV = 2
HD = 64
CONVW = 4
DI = 1536
D = 1024
FFL = 512
TP = 4
HL = H // TP
WI = HL * P_SIZE
CH = WI + 2 * N
L = 256

CZ, CX, CM, CQ, CK, CS, CA = 0, 384, 768, 1024, 1152, 1280, 1408
GAIN_COL = 24
CO, CW, CG, CU, CD, CB = 0, 384, 512, 1024, 1536, 2048

EPS = 1e-05
rope_base = 10000.0
FILL = -1e30
HI = lax.Precision.HIGHEST
MESH = pl.DeviceIdType.MESH
f32 = jnp.float32
bf16 = jnp.bfloat16
VLIMIT = 60 * 1024 * 1024


def nn(a, b, precision=None):
    return lax.dot_general(
        a, b, (((1,), (0,)), ((), ())), precision=precision, preferred_element_type=f32
    )


def nt(a, b, precision=None):
    return lax.dot_general(
        a, b, (((1,), (1,)), ((), ())), precision=precision, preferred_element_type=f32
    )


def tn(a, b, precision=None):
    return lax.dot_general(
        a, b, (((0,), (0,)), ((), ())), precision=precision, preferred_element_type=f32
    )


def rows_of(index, size=L):
    return pl.ds(pl.multiple_of(index * size, size), size)


def remote(src, dst, send, recv, **where):
    return pltpu.make_async_remote_copy(
        src_ref=src,
        dst_ref=dst,
        send_sem=send,
        recv_sem=recv,
        device_id=where,
        device_id_type=MESH,
    )


def iota(shape, dim):
    return lax.broadcasted_iota(jnp.int32, shape, dim)


def loop(n, body):
    lax.fori_loop(0, n, lambda i, c: (body(i), c)[1], 0)


def greet(shards, tp_too, ctx_too=True, shard_too=True):
    barrier = pltpu.get_barrier_semaphore()
    count = 0
    z, c, t = lax.axis_index("shard"), lax.axis_index("ctx"), lax.axis_index("tp")
    if ctx_too:
        pl.semaphore_signal(barrier, inc=1, device_id={"ctx": 1 - c}, device_id_type=MESH)
        count += 1
    if shard_too:

        def one(k):
            pl.semaphore_signal(
                barrier, inc=1, device_id={"shard": lax.rem(z + 1 + k, shards)}, device_id_type=MESH
            )

        loop(shards - 1, one)
        count += shards - 1
    if tp_too:
        for d in range(1, TP):
            pl.semaphore_signal(
                barrier, inc=1, device_id={"tp": lax.rem(t + d, TP)}, device_id_type=MESH
            )
            count += 1
    pl.semaphore_wait(barrier, count)


class Gather:
    def __init__(self, shards, src, dst, zsend, csend, recv, own):
        self.s, self.src, self.dst = shards, src, dst
        self.zsend, self.csend, self.recv, self.own = zsend, csend, recv, own
        self.z, self.c = lax.axis_index("shard"), lax.axis_index("ctx")
        self.r = src.shape[0]

    def block(self, g):
        return self.dst.at[rows_of(g, self.r)]

    def to_shard(self, k):
        g = 2 * self.z + self.c
        return remote(
            self.src,
            self.block(g),
            self.zsend.at[k],
            self.recv.at[g],
            shard=lax.rem(self.z + k, self.s),
        )

    def to_core(self, k):
        zz = lax.rem(self.z + k, self.s)
        g = 2 * zz + self.c
        return remote(self.block(g), self.block(g), self.csend.at[k], self.recv.at[g], ctx=1 - self.c)

    def got(self, k, core):
        zz = lax.rem(self.z + k, self.s)
        g = 2 * zz + core
        return remote(self.block(g), self.block(g), self.csend.at[k], self.recv.at[g], ctx=1 - self.c)

    def start(self):
        keep = pltpu.make_async_copy(self.src, self.block(2 * self.z + self.c), self.own)
        keep.start()
        loop(self.s - 1, lambda k: self.to_shard(k + 1).start())
        keep.wait()
        self.to_core(0).start()

    def forward(self):
        def one(k):
            self.got(k + 1, self.c).wait_recv()
            self.to_core(k + 1).start()

        loop(self.s - 1, one)

    def finish(self):
        loop(self.s, lambda k: self.got(k, 1 - self.c).wait_recv())
        loop(self.s, lambda k: self.to_core(k).wait_send())
        loop(self.s - 1, lambda k: self.to_shard(k + 1).wait_send())

    @staticmethod
    def sems(shards):
        dma = pltpu.SemaphoreType.DMA
        return [dma((shards,)), dma((shards,)), dma((2 * shards,)), dma(())]


class Scatter:
    def __init__(self, shards, src, sib, stage, land, csend, crecv, zsend, zrecv):
        self.s, self.src, self.sib, self.stage, self.land = shards, src, sib, stage, land
        self.csend, self.crecv, self.zsend, self.zrecv = csend, crecv, zsend, zrecv
        self.z, self.c = lax.axis_index("shard"), lax.axis_index("ctx")
        self.r = src.shape[0] // (2 * shards)

    def to_core(self, k):
        zz = lax.rem(self.z + k, self.s)
        return remote(
            self.src.at[rows_of(2 * zz + 1 - self.c, self.r)],
            self.sib.at[zz],
            self.csend.at[zz],
            self.crecv.at[zz],
            ctx=1 - self.c,
        )

    def to_shard(self, k):
        zz = lax.rem(self.z + k, self.s)
        return remote(
            self.stage.at[zz], self.land.at[self.z], self.zsend.at[zz], self.zrecv.at[self.z], shard=zz
        )

    def arrive(self, k):
        zz = lax.rem(self.z + k, self.s)
        return remote(
            self.stage.at[zz], self.land.at[zz], self.zsend.at[zz], self.zrecv.at[zz], shard=zz
        )

    def start(self):
        loop(self.s - 1, lambda k: self.to_core(k + 1).start())
        self.to_core(0).start()

    def middle(self):
        def one(k):
            zz = lax.rem(self.z + 1 + k, self.s)
            self.to_core(k + 1).wait_recv()
            both = self.src[rows_of(2 * zz + self.c, self.r), :].astype(f32)
            self.stage[zz] = (both + self.sib[zz].astype(f32)).astype(bf16)
            self.to_shard(k + 1).start()

        loop(self.s - 1, one)

    def finish(self, out, cols=None):
        self.to_core(0).wait_recv()
        own = self.src[rows_of(2 * self.z + self.c, self.r), :].astype(f32)
        out[...] = own + self.sib[self.z].astype(f32)

        def one(k):
            zz = lax.rem(self.z + 1 + k, self.s)
            self.arrive(k + 1).wait_recv()
            out[...] += self.land[zz].astype(f32)

        loop(self.s - 1, one)
        loop(self.s, lambda k: self.to_core(k).wait_send())
        loop(self.s - 1, lambda k: self.to_shard(k + 1).wait_send())

    @staticmethod
    def scratch(shards, rows, cols):
        dma = pltpu.SemaphoreType.DMA
        block = pltpu.VMEM((shards, rows // (2 * shards), cols), bf16)
        return [block, block, block] + [dma((shards,))] * 4


def sigmoid(v):
    return 1.0 / (1.0 + jnp.exp(-v))


def softplus(v):
    return jnp.maximum(v, 0.0) + jnp.log1p(jnp.exp(-jnp.abs(v)))


def swap_half(v):
    width = v.shape[1]
    low = iota(v.shape, 1) % HD < HD // 2
    return jnp.where(low, pltpu.roll(v, width - HD // 2, 1), pltpu.roll(v, HD // 2, 1))


def low_lanes(shape):
    return iota(shape, 1) < 64


def spread():
    return (iota((N, WI), 1) // P_SIZE == iota((N, WI), 0)).astype(f32)


def first_row():
    return (iota((8, N), 0) == 0).astype(f32)


def wide(column, width):
    return jnp.concatenate([column] * (width // column.shape[1]), axis=1)


def lower_ones():
    return (iota((L, L), 0) >= iota((L, L), 1)).astype(f32)


def project_kernel(shards, hid, wa, wfull, normed, gains, z_out, cin, q_out, kv_out, dt_out, *sems):
    greet(shards, False)
    gather = Gather(shards, wa, wfull, *sems)
    gather.start()
    gather.forward()
    gather.finish()
    turned = wfull[:, CS:CA].astype(f32).T
    gains[...] = turned[GAIN_COL : GAIN_COL + 8]
    gain = gains[0:1, :]

    def block(i):
        rows = rows_of(i)
        x = hid[rows, :].astype(f32)
        scale = lax.rsqrt(jnp.mean(x * x, -1, keepdims=True) + EPS)
        low = (x * scale * gain).astype(bf16)
        normed[rows, :] = low
        z_out[rows, :] = nn(low, wfull[:, CZ:CX])
        cin[rows, :] = nn(low, wfull[:, CX:CQ]).astype(bf16)
        rest = nn(low, wfull[:, CQ:CA])
        q_out[rows, :] = rest[:, : CK - CQ]
        kv_out[rows, :] = rest[:, CK - CQ : CS - CQ]
        dt_out[rows, :] = rest[:, CS - CQ :]

    loop(hid.shape[0] // L, block)


def project(shards, hid, wa):
    t = hid.shape[0]
    out = [
        ((D, CA), bf16),
        ((t, D), bf16),
        ((8, D), f32),
        ((t, WI), f32),
        ((t, CH), bf16),
        ((t, 128), f32),
        ((t, 128), f32),
        ((t, 128), f32),
    ]
    return pl.pallas_call(
        functools.partial(project_kernel, shards),
        out_shape=[jax.ShapeDtypeStruct(*o) for o in out],
        in_specs=[pl.BlockSpec(memory_space=pltpu.VMEM)] * 2,
        out_specs=[pl.BlockSpec(memory_space=pltpu.VMEM)] * len(out),
        scratch_shapes=Gather.sems(shards),
        compiler_params=pltpu.CompilerParams(
            collective_id=0, has_side_effects=True, vmem_limit_bytes=VLIMIT
        ),
        name="project",
    )(hid, wa)


def head_scalars(dt_raw, prm):
    real = iota(dt_raw.shape, 1) < HL
    steps = jnp.where(real, softplus(dt_raw + prm[0:1, :]), 0.0)
    rates = steps * prm[1:2, :]
    return steps, rates


def pair_columns(v, pair):
    return v[:, 128 * pair : 128 * pair + 128]


def own_half(v, half):
    return jnp.where(low_lanes(v.shape) == (half == 0), v, jnp.zeros_like(v))


def forward_kernel(
    shards,
    cin, q_in, kv_in, dt_raw, z_in, cos, sin, wb, taps, prm, chan, length,
    wfull, pre, hist, q_low, kk, vv, att, lse, lse_row, ssd, start, steps_out, cum_out, tot_out,
    gated_low, square,
    pad, act, state, carried, scores_m, scores_l,
    hist_in, zs, cs, gr, own_sem, xs, xr,
):
    c = lax.axis_index("ctx")
    t = cin.shape[0]
    blocks = t // L
    greet(shards, False)
    gather = Gather(shards, wb, wfull, zs, cs, gr, own_sem)
    gather.start()

    def swap(src, dst, i):
        return remote(src, dst, xs.at[i], xr.at[i], ctx=1 - c)

    tail = swap(cin.at[pl.ds(t - 16, 16)], hist_in, 0)
    tail.start()
    low128 = low_lanes((L, 128))

    def rotary(i):
        rows = rows_of(i)
        cosine, sine = cos[rows, :], sin[rows, :]
        v = q_in[rows, :]
        q_low[rows, :] = (v * cosine + swap_half(v) * sine).astype(bf16)
        v = kv_in[rows, :]
        other = pltpu.roll(v, 64, 1)
        twice = jnp.where(low128, v, other)
        kk[0, rows, :] = (twice * cosine + swap_half(twice) * sine).astype(bf16)
        vv[0, rows, :] = jnp.where(low128, other, v).astype(bf16)

    loop(blocks, rotary)
    keys = swap(kk.at[0], kk.at[1], 1)
    keys.start()
    vals = swap(vv.at[0], vv.at[1], 2)
    vals.start()

    tail.wait_recv()
    before = hist_in[8:16, :].astype(f32)
    hist[...] = jnp.where((iota((8, CH), 0) >= 5) & (c > 0), before, 0.0)
    pad[0:8, :] = hist[...]

    def fill(i):
        pad[pl.ds(pl.multiple_of(i * L + 8, 8), L), :] = cin[rows_of(i), :].astype(f32)

    loop(blocks, fill)
    ones = lower_ones()
    expand = spread()
    state[...] = jnp.zeros_like(state)

    for i in range(blocks):
        rows = pl.ds(i * L, L)
        v = taps[4:5, :] + taps[0:1, :] * pad[pl.ds(i * L + 5, L), :]
        for j in range(1, CONVW):
            v = v + taps[j : j + 1, :] * pad[pl.ds(i * L + 5 + j, L), :]
        pre[rows, :] = v
        a = v * sigmoid(v)
        act[rows, :] = a
        steps, rates = head_scalars(dt_raw[rows, :], prm)
        cum = nn(ones, rates, HI)
        tot = cum[L - 1 : L, :]
        steps_out[rows, :] = steps
        cum_out[rows, :] = cum
        tot_out[i] = jnp.broadcast_to(tot, (8, 128))
        weight = nn(jnp.exp(tot - cum) * steps, expand, HI)
        start[i] = state[...]
        add = tn(a[:, WI : WI + N].astype(bf16), (weight * a[:, :WI]).astype(bf16))
        decay = nn(jnp.broadcast_to(jnp.exp(tot), (8, 128)), expand, HI)[0:1, :]
        state[...] = decay * state[...] + add

    states = swap(state, carried, 3)
    states.start()
    gather.forward()

    keys.wait_recv()
    vals.wait_recv()
    scale = HD ** (-0.5)
    limit = length[0] - c * t

    def stacked(v):
        return jnp.concatenate([own_half(v, 0), own_half(v, 1)], axis=0)

    for i in range(blocks):
        rows = pl.ds(i * L, L)
        width = (i + 1) * L
        q2 = stacked(q_low[rows, :].astype(f32)).astype(bf16)
        s = nt(q2, kk[0, 0:width, :]) * scale
        at = iota(s.shape, 0) % L + i * L
        col = iota(s.shape, 1)
        s = jnp.where((col <= at) & (col < limit), s, FILL)
        peak = jnp.max(s, -1, keepdims=True)
        e = jnp.exp(s - peak)
        total = jnp.sum(e, -1, keepdims=True)
        o = nn(e.astype(bf16), vv[0, 0:width, :])
        scores_m[...] = jnp.broadcast_to(peak, (2 * L, 128))
        scores_l[0] = jnp.broadcast_to(total, (2 * L, 128))
        scores_l[1] = o

        @pl.when(c > 0)
        def earlier():
            s2 = nt(q2, kk[1]) * scale
            old = scores_m[:, 0:1]
            new = jnp.maximum(old, jnp.max(s2, -1, keepdims=True))
            e2 = jnp.exp(s2 - new)
            fade = jnp.exp(old - new)
            scores_m[...] = jnp.broadcast_to(new, (2 * L, 128))
            scores_l[0] = fade * scores_l[0] + jnp.sum(e2, -1, keepdims=True)
            scores_l[1] = fade * scores_l[1] + nn(e2.astype(bf16), vv[1])

        total = scores_l[0]
        o = scores_l[1] / total
        att[rows, :] = jnp.where(low128, o[:L], o[L:])
        logs = scores_m[...] + jnp.log(total)
        both = jnp.where(low128, logs[:L], logs[L:])
        lse[rows, :] = both
        turned = both.T
        lse_row[0:1, rows] = turned[0:1]
        lse_row[1:2, rows] = turned[64:65]
        lse_row[2:8, rows] = jnp.zeros((6, L), f32)

    states.wait_recv()
    carried[...] = jnp.where(c > 0, carried[...], 0.0)
    mask = iota((L, L), 0) >= iota((L, L), 1)
    for i in range(blocks):
        rows = pl.ds(i * L, L)
        if i > 0:
            decay = nn(jnp.exp(tot_out[i - 1]), expand, HI)[0:1, :]
            carried[...] = carried[...] * decay
        start[i] = start[i] + carried[...]
        s0 = start[i].astype(bf16)
        steps, cum = steps_out[rows, :], cum_out[rows, :]
        x = act[rows, 0:WI]
        xl = x.astype(bf16)
        in_map = act[rows, WI : WI + N].astype(bf16)
        out_map = act[rows, WI + N : CH].astype(bf16)
        gram = nt(out_map, in_map)
        cum_t, steps_t = cum.T, steps.T
        inner = []
        for pair in range(HL // 2):
            halves = []
            for half in range(2):
                h = 2 * pair + half
                decay = jnp.exp(jnp.where(mask, cum[:, h : h + 1] - cum_t[h : h + 1, :], FILL))
                mixing = gram * decay * steps_t[h : h + 1, :]
                halves.append(nn(mixing.astype(bf16), pair_columns(xl, pair)))
            inner.append(jnp.where(low128, halves[0], halves[1]))
        y = jnp.concatenate(inner, axis=1)
        y = y + nn(jnp.exp(cum), expand, HI) * nn(out_map, s0) + chan[1:2, :] * x
        ssd[rows, :] = y
        zz = z_in[rows, :]
        gated = y * zz * sigmoid(zz)
        gated_low[rows, :] = (gated * chan[0:1, :]).astype(bf16)
        square[:, rows] = nt(jnp.ones((8, WI), f32), gated * gated, HI)

    gather.finish()
    for copy in (tail, keys, vals, states):
        copy.wait_send()


def forward(shards, cin, q, kv, dt, z, cos, sin, wb, taps, prm, chan, length):
    t = cin.shape[0]
    out = [
        ((D, CB), bf16),
        ((t, CH), f32),
        ((8, CH), f32),
        ((t, 128), bf16),
        ((2, t, 128), bf16),
        ((2, t, 128), bf16),
        ((t, 128), f32),
        ((t, 128), f32),
        ((8, t), f32),
        ((t, WI), f32),
        ((t // L, N, WI), f32),
        ((t, 128), f32),
        ((t, 128), f32),
        ((t // L, 8, 128), f32),
        ((t, WI), bf16),
        ((8, t), f32),
    ]
    dma = pltpu.SemaphoreType.DMA
    vmem = pl.BlockSpec(memory_space=pltpu.VMEM)
    return pl.pallas_call(
        functools.partial(forward_kernel, shards),
        out_shape=[jax.ShapeDtypeStruct(*o) for o in out],
        in_specs=[vmem] * 11 + [pl.BlockSpec(memory_space=pltpu.SMEM)],
        out_specs=[vmem] * len(out),
        scratch_shapes=[
            pltpu.VMEM((t + 8, CH), f32),
            pltpu.VMEM((t, CH), f32),
            pltpu.VMEM((N, WI), f32),
            pltpu.VMEM((N, WI), f32),
            pltpu.VMEM((2 * L, 128), f32),
            pltpu.VMEM((2, 2 * L, 128), f32),
            pltpu.VMEM((16, CH), bf16),
        ]
        + Gather.sems(shards)
        + [dma((4,)), dma((4,))],
        compiler_params=pltpu.CompilerParams(
            collective_id=1, has_side_effects=True, vmem_limit_bytes=VLIMIT
        ),
        name="mix_forward",
    )(cin, q, kv, dt, z, cos, sin, wb, taps, prm, chan, length)


def ffn_kernel(
    hid, cot, gl, att, square, wb, gains, length,
    output, grad_own, grads, gain_grad, total_square, ggl, grad_att, dots,
    grad_res, partial, seed, send1, recv1, low_two, grad_act, act, gg, gu, gown,
    unit, scale_keep, osend, orecv, gsend, grecv, sqall,
    sqs, sqr, s1, r1, ns, nr, os, orr, gs, gr, hs, hr,
):
    t = hid.shape[0]
    tp, c = lax.axis_index("tp"), lax.axis_index("ctx")
    chunk = t // TP
    width = D // TP
    greet(1, True, False, False)

    def peer(d):
        return lax.rem(tp + d, TP)

    def crow(i):
        return rows_of(i, chunk)

    def square_to(d):
        return remote(sqall.at[tp], sqall.at[tp], sqs.at[d], sqr.at[tp], tp=peer(d))

    def square_from(d):
        return remote(sqall.at[tp], sqall.at[peer(d)], sqs.at[d], sqr.at[peer(d)], tp=peer(d))

    sqall[tp] = square[...]
    for d in range(1, TP):
        square_to(d).start()
    limit = length[0] - c * t

    def mask_seed(i):
        rows = crow(i)
        live = iota((chunk, D), 0) + i * chunk < limit
        seed[rows, :] = jnp.where(live, cot[rows, :].astype(f32), 0.0).astype(bf16)

    loop(TP, mask_seed)
    for d in range(1, TP):
        square_from(d).wait_recv()
    total_square[...] = sqall[0] + sqall[1] + sqall[2] + sqall[3]

    def first_to(d):
        return remote(send1.at[d], recv1.at[tp], s1.at[d], r1.at[tp], tp=peer(d))

    def first_from(d):
        return remote(send1.at[d], recv1.at[peer(d)], s1.at[d], r1.at[peer(d)], tp=peer(d))

    def mix(k):
        d = lax.rem(k + 1, TP)
        rows = crow(peer(d))
        scale = lax.rsqrt(total_square[:, rows] / DI + EPS)
        column = wide(tn(scale, first_row(), HI), D)
        both = nt(gl[rows, :], wb[:, CO:CW]) * column + nt(att[rows, :], wb[:, CW:CG])
        partial[rows, :] = both

        @pl.when(d > 0)
        def go():
            send1[d] = both.astype(bf16)
            first_to(d).start()

    loop(TP, mix)

    def act_grad(i):
        rows = crow(i)
        grad_act[rows, :] = nn(seed[rows, :], wb[:, CD:CB])

    loop(TP, act_grad)
    for d in range(1, TP):
        first_from(d).wait_recv()
    own = crow(tp)
    acc = hid[own, :].astype(f32) + partial[own, :]
    for d in range(1, TP):
        acc = acc + recv1[peer(d)].astype(f32)
    scale = lax.rsqrt(jnp.mean(acc * acc, -1, keepdims=True) + EPS)
    scale_keep[...] = jnp.broadcast_to(scale, scale_keep.shape)
    unit[...] = acc * scale
    gain = gains[1:2, :]
    low_two[own, :] = (unit[...] * gain).astype(bf16)

    def norm_to(d):
        return remote(low_two.at[own], low_two.at[own], ns.at[d], nr.at[tp], tp=peer(d))

    def norm_from(d):
        there = low_two.at[crow(peer(d))]
        return remote(there, there, ns.at[d], nr.at[peer(d)], tp=peer(d))

    for d in range(1, TP):
        norm_to(d).start()

    def grad_to(d):
        return remote(gsend.at[d], grecv.at[tp], gs.at[d], gr.at[tp], tp=peer(d))

    def grad_from(d):
        return remote(gsend.at[d], grecv.at[peer(d)], gs.at[d], gr.at[peer(d)], tp=peer(d))

    def out_to(e, i):
        rows = crow(i)
        return remote(
            osend.at[e, rows], orecv.at[tp, rows], os.at[e, i], orr.at[tp, i], tp=peer(e)
        )

    def out_from(e, i):
        rows = crow(i)
        return remote(
            osend.at[e, rows], orecv.at[peer(e), rows], os.at[e, i], orr.at[peer(e), i], tp=peer(e)
        )

    def hidden_units(d):
        i = peer(d)
        rows = crow(i)

        @pl.when(d > 0)
        def arrive():
            norm_from(d).wait_recv()

        low = low_two[rows, :]
        gate, up = nn(low, wb[:, CG:CU]), nn(low, wb[:, CU:CD])
        sig = sigmoid(gate)
        silu = gate * sig
        hidden_act = (silu * up).astype(bf16)
        act[rows, :] = hidden_act
        ga = grad_act[rows, :]
        g1 = (ga * up * (sig * (1.0 + gate * (1.0 - sig)))).astype(bf16)
        g2 = (ga * silu).astype(bf16)
        gg[rows, :] = g1
        gu[rows, :] = g2
        back = nt(g1, wb[:, CG:CU]) + nt(g2, wb[:, CU:CD])

        @pl.when(d > 0)
        def go():
            gsend[d] = back.astype(bf16)
            grad_to(d).start()

        @pl.when(d == 0)
        def keep():
            gown[...] = back

        partial[rows, :] = partial[rows, :] + nt(hidden_act, wb[:, CD:CB])
        for e in range(1, TP):
            osend[e, rows, :] = partial[rows, rows_of(peer(e), width)].astype(bf16)
            out_to(e, i).start()

    loop(TP, hidden_units)

    def weight_grads(i):
        feats = rows_of(i)
        low = low_two[:, feats]
        grads[feats, CG:CU] = tn(low, gg[...]).astype(bf16)
        grads[feats, CU:CD] = tn(low, gu[...]).astype(bf16)

    loop(D // L, weight_grads)
    for d in range(1, TP):
        grad_from(d).wait_recv()
    back = gown[...]
    for d in range(1, TP):
        back = back + grecv[peer(d)].astype(f32)
    gain_grad[...] = jnp.broadcast_to(jnp.sum(back * unit[...], 0, keepdims=True), (8, D))
    weighted = back * gain
    mean = jnp.mean(weighted * unit[...], -1, keepdims=True)
    res = seed[own, :].astype(f32) + scale_keep[:, 0:1] * (weighted - unit[...] * mean)
    grad_own[...] = res
    grad_res[own, :] = res.astype(bf16)

    def res_to(d):
        return remote(grad_res.at[own], grad_res.at[own], hs.at[d], hr.at[tp], tp=peer(d))

    def res_from(d):
        there = grad_res.at[crow(peer(d))]
        return remote(there, there, hs.at[d], hr.at[peer(d)], tp=peer(d))

    for d in range(1, TP):
        res_to(d).start()

    def down_grads(i):
        feats = rows_of(i)
        grads[feats, CD:CB] = tn(seed[:, feats], act[...]).astype(bf16)

    loop(D // L, down_grads)
    for d in range(1, TP):
        for i in range(TP):
            out_from(d, i).wait_recv()
    mine = rows_of(tp, width)
    total = hid[:, mine].astype(f32) + partial[:, mine]
    for d in range(1, TP):
        total = total + orecv[peer(d)].astype(f32)
    output[...] = total.astype(bf16)
    for d in range(1, TP):
        norm_to(d).wait_send()

    def out_back(d):
        i = peer(d)
        rows = crow(i)

        @pl.when(d > 0)
        def arrive():
            res_from(d).wait_recv()

        square_scale = lax.rsqrt(total_square[:, rows] / DI + EPS)
        column = wide(tn(square_scale, first_row(), HI), D)
        got = grad_res[rows, :]
        proj = (column * got.astype(f32)).astype(bf16)
        low_two[rows, :] = proj
        product = nn(proj, wb[:, CO:CW])
        ggl[rows, :] = product
        dots[:, rows] = nt(jnp.ones((8, WI), f32), product * gl[rows, :].astype(f32), HI)
        grad_att[rows, :] = nn(got, wb[:, CW:CG]).astype(bf16)

    loop(TP, out_back)

    def out_grads(i):
        feats = rows_of(i)
        grads[feats, CO:CW] = tn(low_two[:, feats], gl[...]).astype(bf16)
        grads[feats, CW:CG] = tn(grad_res[:, feats], att[...]).astype(bf16)

    loop(D // L, out_grads)
    for d in range(1, TP):
        square_to(d).wait_send()
        first_to(d).wait_send()
        grad_to(d).wait_send()
        res_to(d).wait_send()
        for i in range(TP):
            out_to(d, i).wait_send()


def ffn(hid, cot, gl, att, square, wb, gains, length):
    t = hid.shape[0]
    chunk = t // TP
    out = [
        ((t, D // TP), bf16),
        ((chunk, D), f32),
        ((D, CB), bf16),
        ((8, D), f32),
        ((8, t), f32),
        ((t, WI), f32),
        ((t, 128), bf16),
        ((8, t), f32),
    ]
    dma = pltpu.SemaphoreType.DMA
    vmem = pl.BlockSpec(memory_space=pltpu.VMEM)
    return pl.pallas_call(
        ffn_kernel,
        out_shape=[jax.ShapeDtypeStruct(*o) for o in out],
        in_specs=[vmem] * 7 + [pl.BlockSpec(memory_space=pltpu.SMEM)],
        out_specs=[vmem] * len(out),
        scratch_shapes=[
            pltpu.VMEM((t, D), bf16),
            pltpu.VMEM((t, D), f32),
            pltpu.VMEM((t, D), bf16),
            pltpu.VMEM((TP, chunk, D), bf16),
            pltpu.VMEM((TP, chunk, D), bf16),
            pltpu.VMEM((t, D), bf16),
            pltpu.VMEM((t, FFL), f32),
            pltpu.VMEM((t, FFL), bf16),
            pltpu.VMEM((t, FFL), bf16),
            pltpu.VMEM((t, FFL), bf16),
            pltpu.VMEM((chunk, D), f32),
            pltpu.VMEM((chunk, D), f32),
            pltpu.VMEM((chunk, 128), f32),
            pltpu.VMEM((TP, t, D // TP), bf16),
            pltpu.VMEM((TP, t, D // TP), bf16),
            pltpu.VMEM((TP, chunk, D), bf16),
            pltpu.VMEM((TP, chunk, D), bf16),
            pltpu.VMEM((TP, 8, t), f32),
        ]
        + [dma((TP,))] * 6
        + [dma((TP, TP))] * 2
        + [dma((TP,))] * 4,
        compiler_params=pltpu.CompilerParams(
            collective_id=2, has_side_effects=True, vmem_limit_bytes=VLIMIT
        ),
        name="feed_forward",
    )(hid, cot, gl, att, square, wb, gains, length)


def backward_kernel(
    shards,
    ggl, grad_att, dots_in, total_square, grads,
    pre, cin, hist, q_low, kk, vv, att, lse_row, ssd, start, steps_in, cum_in, tot_in, dt_raw, z_in,
    cos, sin, taps, prm, chan, length,
    lin, grad_b, conv_grads, chan_grads, head_grads,
    dots, dk, dv, dy, dpre, ends, dstate, carry, kv_out, kv_in, pad, edge_out, edge_in,
    sib, stage, land, csend, crecv, zsend, zrecv, xs, xr, ts, tr,
):
    c, tp = lax.axis_index("ctx"), lax.axis_index("tp")
    t = cin.shape[0]
    blocks = t // L
    greet(shards, True)
    scatter = Scatter(shards, grads, sib, stage, land, csend, crecv, zsend, zrecv)
    scatter.start()

    def swap(src, dst, i):
        return remote(src, dst, xs.at[i], xr.at[i], ctx=1 - c)

    def peer(d):
        return lax.rem(tp + d, TP)

    def dot_to(d):
        return remote(dots.at[tp], dots.at[tp], ts.at[d], tr.at[tp], tp=peer(d))

    def dot_from(d):
        return remote(dots.at[tp], dots.at[peer(d)], ts.at[d], tr.at[peer(d)], tp=peer(d))

    dots[tp] = dots_in[...]
    for d in range(1, TP):
        dot_to(d).start()
    expand = spread()
    low128 = low_lanes((L, 128))
    chan_grads[...] = jnp.zeros_like(chan_grads)
    head_grads[...] = jnp.zeros_like(head_grads)
    conv_grads[...] = jnp.zeros_like(conv_grads)
    for d in range(1, TP):
        dot_from(d).wait_recv()

    def gated_back(i):
        rows = rows_of(i)
        both = dots[0, :, rows] + dots[1, :, rows] + dots[2, :, rows] + dots[3, :, rows]
        share = both / ((total_square[:, rows] / DI + EPS) * DI)
        column = wide(tn(share, first_row(), HI), WI)
        zz, y = z_in[rows, :], ssd[rows, :]
        sig = sigmoid(zz)
        silu = zz * sig
        gated = y * silu
        product = ggl[rows, :]
        chan_grads[0:1, :] += jnp.sum(product * gated, 0, keepdims=True)
        grad_gated = product * chan[0:1, :] - column * gated
        grad_y = grad_gated * silu
        dy[rows, :] = grad_y
        lin[rows, CZ:CX] = (grad_gated * y * (sig * (1.0 + zz * (1.0 - sig)))).astype(bf16)
        v = pre[rows, WI + N : CH]
        out_map = (v * sigmoid(v)).astype(bf16)
        ends[i] = tn(out_map, (nn(jnp.exp(cum_in[rows, :]), expand, HI) * grad_y).astype(bf16))

    loop(blocks, gated_back)
    dstate[...] = jnp.zeros_like(dstate)

    def chain(k):
        i = blocks - 1 - k
        add = ends[i]
        ends[i] = dstate[...]
        dstate[...] = nn(jnp.exp(tot_in[i]), expand, HI)[0:1, :] * dstate[...] + add

    loop(blocks, chain)
    states = swap(dstate, carry, 0)
    states.start()
    scatter.middle()

    scale = HD ** (-0.5)
    limit = length[0] - c * t
    dk[...] = jnp.zeros_like(dk)
    dv[...] = jnp.zeros_like(dv)
    head_of = ((iota((8, 128), 1) // HD) == iota((8, 128), 0)).astype(f32)

    def stacked(v):
        return jnp.concatenate([own_half(v, 0), own_half(v, 1)], axis=0).astype(bf16)

    def side_by_side(v):
        return jnp.concatenate([v[0:1, :], v[1:2, :]], axis=1)

    for i in range(blocks):
        rows = pl.ds(i * L, L)
        width = (i + 1) * L
        q2 = stacked(q_low[rows, :].astype(f32))
        go = grad_att[rows, :].astype(f32)
        go2 = stacked(go)
        row_dot = side_by_side(nt(head_of, go * att[rows, :], HI))
        logs = side_by_side(lse_row[:, rows])
        turn = cos[rows, :], sin[rows, :]

        def keys_of(part, size, masked):
            k, v = kk[part, 0:size, :], vv[part, 0:size, :]
            s = nt(k, q2) * scale - logs
            if masked:
                at = iota(s.shape, 1) % L + i * L
                row = iota(s.shape, 0)
                s = jnp.where((row <= at) & (row < limit), s, FILL)
            p = jnp.exp(s)
            ds = (p * (nt(v, go2) - row_dot)).astype(bf16)
            dv[part, 0:size, :] += nn(p.astype(bf16), go2)
            dk[part, 0:size, :] += nn(ds, q2)
            out = tn(ds, k) * scale
            out = jnp.where(low128, out[:L], out[L:])
            return out * turn[0] - swap_half(out) * turn[1]

        pad[rows, 0:128] = keys_of(0, width, True)

        @pl.when(c > 0)
        def earlier():
            pad[rows, 0:128] += keys_of(1, t, False)

        lin[rows, CQ:CK] = pad[rows, 0:128].astype(bf16)

    def key_values(part, rows):
        gk, gv = dk[part, rows, :] * scale, dv[part, rows, :]
        return jnp.where(low128, gk + pltpu.roll(gk, 64, 1), gv + pltpu.roll(gv, 64, 1))

    def pack(i):
        rows = rows_of(i)
        kv_out[rows, :] = key_values(1, rows).astype(bf16)

    loop(blocks, pack)
    pairs = swap(kv_out, kv_in, 1)
    pairs.start()

    pad[0:8, :] = hist[...]

    def fill(i):
        pad[pl.ds(pl.multiple_of(i * L + 8, 8), L), :] = cin[rows_of(i), :].astype(f32)

    loop(blocks, fill)
    states.wait_recv()
    carry[...] = jnp.where(c == 0, carry[...], 0.0)

    def add_carry(k):
        i = blocks - 1 - k
        ends[i] = ends[i] + carry[...]
        carry[...] = nn(jnp.exp(tot_in[i]), expand, HI)[0:1, :] * carry[...]

    loop(blocks, add_carry)
    mask = iota((L, L), 0) >= iota((L, L), 1)
    ones = lower_ones()
    lane = iota((L, 128), 1)

    def fold(v):
        return nt(v, expand, HI)

    def scan_back(i):
        rows = rows_of(i)
        v = pre[rows, :]
        sig = sigmoid(v)
        a = v * sig
        x = a[:, :WI]
        xl, bl, cl = x.astype(bf16), a[:, WI : WI + N].astype(bf16), a[:, WI + N :].astype(bf16)
        steps, cum = steps_in[rows, :], cum_in[rows, :]
        tot = cum[L - 1 : L, :]
        ecum, wend = jnp.exp(cum), jnp.exp(tot - cum)
        weight = wend * steps
        ecum_x, weight_x = nn(ecum, expand, HI), nn(weight, expand, HI)
        grad_y = dy[rows, :]
        dyl = grad_y.astype(bf16)
        s0, d1 = start[i], ends[i]
        s0l, d1l = s0.astype(bf16), d1.astype(bf16)
        bd, cs = nn(bl, d1l), nn(cl, s0l)
        dw = fold(x * bd)
        crossing = jnp.broadcast_to(jnp.sum(s0 * d1, 0, keepdims=True), (8, WI))
        dtot = jnp.sum(weight * dw, 0, keepdims=True) + jnp.exp(tot) * fold(crossing)[0:1, :]
        gram = nt(cl, bl)
        cum_t, steps_t = cum.T, steps.T
        dgram = jnp.zeros((L, L), f32)
        row_sums = jnp.zeros((L, 128), f32)
        col_sums, inner = [], []
        for pair in range(HL // 2):
            xp, dp = pair_columns(xl, pair), pair_columns(dyl, pair)
            dpf = pair_columns(grad_y, pair)
            halves = []
            for half in range(2):
                h = 2 * pair + half
                decay = jnp.exp(jnp.where(mask, cum[:, h : h + 1] - cum_t[h : h + 1, :], FILL))
                q = nt(own_half(dpf, half).astype(bf16), xp)
                mixed = gram * decay
                srow = steps_t[h : h + 1, :]
                f = mixed * q
                col_sums.append(jnp.sum(f, 0, keepdims=True))
                row_sums = jnp.where(lane == h, jnp.sum(f * srow, -1, keepdims=True), row_sums)
                dgram = dgram + decay * srow * q
                halves.append(tn((mixed * srow).astype(bf16), dp))
            inner.append(jnp.where(low128, halves[0], halves[1]))
        cols = jnp.concatenate(col_sums + [jnp.zeros((128 - HL, L), f32)], axis=0).T
        dcum = fold(grad_y * cs) * ecum - weight * dw + row_sums - steps * cols
        dcum = dcum + jnp.where(iota((L, 128), 0) == L - 1, dtot, 0.0)
        drate = tn(ones, dcum, HI)
        rate_of = prm[1:2, :]
        raw = dt_raw[rows, :] + prm[0:1, :]
        dstep = (wend * dw + cols + drate * rate_of) * sigmoid(raw)
        dstep = jnp.where(lane < HL, dstep, 0.0)
        lin[rows, CS:CA] = dstep.astype(bf16)
        head_grads[0:1, :] += jnp.sum(dstep, 0, keepdims=True)
        head_grads[1:2, :] += jnp.sum(drate * steps * rate_of, 0, keepdims=True)
        head_grads[2:3, :] += jnp.sum(fold(grad_y * x), 0, keepdims=True)
        slope = sig * (1.0 + v * (1.0 - sig))
        dx = chan[1:2, :] * grad_y + weight_x * bd + jnp.concatenate(inner, axis=1)
        dg = dgram.astype(bf16)
        db = tn(dg, cl) + nt((weight_x * x).astype(bf16), d1l)
        dc = nn(dg, bl) + nt((ecum_x * grad_y).astype(bf16), s0l)
        dpre[rows, 0:WI] = dx * slope[:, :WI]
        dpre[rows, WI : WI + N] = db * slope[:, WI : WI + N]
        dpre[rows, WI + N : CH] = dc * slope[:, WI + N :]

    loop(blocks, scan_back)
    edge_out[...] = dpre[0:8, :]
    edge = swap(edge_out, edge_in, 2)
    edge.start()
    pairs.wait_recv()

    def keys_back(i):
        rows = rows_of(i)
        v = key_values(0, rows) + kv_in[rows, :].astype(f32)
        cosine = jnp.where(low128, cos[rows, :], 1.0)
        sine = jnp.where(low128, sin[rows, :], 0.0)
        lin[rows, CK:CS] = (v * cosine - swap_half(v) * sine).astype(bf16)

    loop(blocks, keys_back)
    edge.wait_recv()
    dpre[pl.ds(t, 8), :] = jnp.where(c == 0, edge_in[...], 0.0)
    for i in range(blocks):
        rows = pl.ds(i * L, L)
        g = dpre[rows, :]
        conv_grads[4:5, :] += jnp.sum(g, 0, keepdims=True)
        back = jnp.zeros_like(g)
        for j in range(CONVW):
            back = back + taps[j : j + 1, :] * dpre[pl.ds(i * L + CONVW - 1 - j, L), :]
            conv_grads[j : j + 1, :] += jnp.sum(g * pad[pl.ds(i * L + 5 + j, L), :], 0, keepdims=True)
        lin[rows, CX:CQ] = back.astype(bf16)
    scatter.finish(grad_b)
    for copy in (states, pairs, edge):
        copy.wait_send()
    for d in range(1, TP):
        dot_to(d).wait_send()


def backward(shards, *args):
    t = args[6].shape[0]
    rows = D // (2 * shards)
    out = [
        ((t, CA), bf16),
        ((rows, CB), f32),
        ((8, CH), f32),
        ((8, WI), f32),
        ((8, 128), f32),
    ]
    dma = pltpu.SemaphoreType.DMA
    vmem = pl.BlockSpec(memory_space=pltpu.VMEM)
    return pl.pallas_call(
        functools.partial(backward_kernel, shards),
        out_shape=[jax.ShapeDtypeStruct(*o) for o in out],
        in_specs=[vmem] * (len(args) - 1) + [pl.BlockSpec(memory_space=pltpu.SMEM)],
        out_specs=[vmem] * len(out),
        scratch_shapes=[
            pltpu.VMEM((TP, 8, t), f32),
            pltpu.VMEM((2, t, 128), f32),
            pltpu.VMEM((2, t, 128), f32),
            pltpu.VMEM((t, WI), f32),
            pltpu.VMEM((t + 8, CH), f32),
            pltpu.VMEM((t // L, N, WI), f32),
            pltpu.VMEM((N, WI), f32),
            pltpu.VMEM((N, WI), f32),
            pltpu.VMEM((t, 128), bf16),
            pltpu.VMEM((t, 128), bf16),
            pltpu.VMEM((t + 8, CH), f32),
            pltpu.VMEM((8, CH), f32),
            pltpu.VMEM((8, CH), f32),
        ]
        + Scatter.scratch(shards, D, CB)
        + [dma((3,)), dma((3,)), dma((TP,)), dma((TP,))],
        compiler_params=pltpu.CompilerParams(
            collective_id=3, has_side_effects=True, vmem_limit_bytes=VLIMIT
        ),
        name="mix_backward",
    )(*args)


def finish_kernel(
    shards,
    lin, normed, wfull, hid, grad_own, gains, gain_two,
    grad_hidden, grad_a, shared,
    gsend, grecv, gown, grads, misc, misc_low, misc_sum, low, shsend,
    sib, stage, land, csend, crecv, zsend, zrecv,
    sib2, stage2, land2, csend2, crecv2, zsend2, zrecv2,
    gs, gr, hs, hr, ss, sr,
):
    tp = lax.axis_index("tp")
    t = lin.shape[0]
    chunk = t // TP
    greet(shards, True)
    scatter = Scatter(shards, grads, sib, stage, land, csend, crecv, zsend, zrecv)
    small = Scatter(shards, misc_low, sib2, stage2, land2, csend2, crecv2, zsend2, zrecv2)

    def peer(d):
        return lax.rem(tp + d, TP)

    def crow(i):
        return rows_of(i, chunk)

    def grad_to(d):
        return remote(gsend.at[d], grecv.at[tp], gs.at[d], gr.at[tp], tp=peer(d))

    def grad_from(d):
        return remote(gsend.at[d], grecv.at[peer(d)], gs.at[d], gr.at[peer(d)], tp=peer(d))

    def product(k):
        d = lax.rem(k + 1, TP)
        back = nt(lin[crow(peer(d)), :], wfull[...])

        @pl.when(d > 0)
        def go():
            gsend[d] = back.astype(bf16)
            grad_to(d).start()

        @pl.when(d == 0)
        def keep():
            gown[...] = back

    loop(TP, product)

    def weight_grads(i):
        feats = rows_of(i)
        both = tn(normed[:, feats], lin[...])
        grads[feats, :] = both[:, :CS].astype(bf16)
        misc[feats, :] = both[:, CS:]

    loop(D // L, weight_grads)
    scatter.start()
    for d in range(1, TP):
        grad_from(d).wait_recv()
    own = crow(tp)
    back = gown[...]
    for d in range(1, TP):
        back = back + grecv[peer(d)].astype(f32)
    x = hid[own, :].astype(f32)
    scale = lax.rsqrt(jnp.mean(x * x, -1, keepdims=True) + EPS)
    unit = x * scale
    gain_one = jnp.broadcast_to(jnp.sum(back * unit, 0, keepdims=True), (8, D))
    weighted = back * gains[0:1, :]
    mean = jnp.mean(weighted * unit, -1, keepdims=True)
    low[own, :] = (grad_own[...] + scale * (weighted - unit * mean)).astype(bf16)

    def low_to(d):
        return remote(low.at[own], low.at[own], hs.at[d], hr.at[tp], tp=peer(d))

    def low_from(d):
        there = low.at[crow(peer(d))]
        return remote(there, there, hs.at[d], hr.at[peer(d)], tp=peer(d))

    for d in range(1, TP):
        low_to(d).start()
    gain_rows = jnp.where(iota((8, D), 0) == 0, gain_one, gain_two[...])
    row, lane = iota((8, 128), 0), iota((8, 128), 1)
    pick = ((row < 2) & (lane == GAIN_COL + row)).astype(f32)
    misc_low[...] = (misc[...] + tn(gain_rows, pick, HI)).astype(bf16)
    small.start()
    scatter.middle()
    small.middle()
    grad_hidden[own, :] = low[own, :].astype(f32)
    for d in range(1, TP):
        low_from(d).wait_recv()
        rows = crow(peer(d))
        grad_hidden[rows, :] = low[rows, :].astype(f32)
    scatter.finish(grad_a)
    small.finish(misc_sum)
    part = grad_a.shape[0] // TP
    for i in range(TP):
        shsend[i, :, 0:256] = grad_a[i * part : (i + 1) * part, CM:CQ]
        shsend[i, :, 256:384] = grad_a[i * part : (i + 1) * part, CK:CS]
        shsend[i, :, 384:512] = misc_sum[i * part : (i + 1) * part, :]

    def share_to(d):
        return remote(shsend.at[peer(d)], shared.at[tp], ss.at[d], sr.at[tp], tp=peer(d))

    def share_from(d):
        return remote(shsend.at[peer(d)], shared.at[peer(d)], ss.at[d], sr.at[peer(d)], tp=peer(d))

    for d in range(1, TP):
        share_to(d).start()
    shared[tp] = shsend[tp]
    for d in range(1, TP):
        share_from(d).wait_recv()
    for d in range(1, TP):
        share_to(d).wait_send()
        grad_to(d).wait_send()
        low_to(d).wait_send()


def finish(shards, *args):
    t = args[0].shape[0]
    rows = D // (2 * shards)
    chunk = t // TP
    out = [((t, D), f32), ((rows, CS), f32), ((TP, rows // TP, 512), f32)]
    dma = pltpu.SemaphoreType.DMA
    vmem = pl.BlockSpec(memory_space=pltpu.VMEM)
    return pl.pallas_call(
        functools.partial(finish_kernel, shards),
        out_shape=[jax.ShapeDtypeStruct(*o) for o in out],
        in_specs=[vmem] * len(args),
        out_specs=[vmem] * len(out),
        scratch_shapes=[
            pltpu.VMEM((TP, chunk, D), bf16),
            pltpu.VMEM((TP, chunk, D), bf16),
            pltpu.VMEM((chunk, D), f32),
            pltpu.VMEM((D, CS), bf16),
            pltpu.VMEM((D, 128), f32),
            pltpu.VMEM((D, 128), bf16),
            pltpu.VMEM((rows, 128), f32),
            pltpu.VMEM((t, D), bf16),
            pltpu.VMEM((TP, rows // TP, 512), f32),
        ]
        + Scatter.scratch(shards, D, CS)
        + Scatter.scratch(shards, D, 128)
        + [dma((TP,))] * 6,
        compiler_params=pltpu.CompilerParams(
            collective_id=4, has_side_effects=True, vmem_limit_bytes=VLIMIT
        ),
        name="project_backward",
    )(*args)


def rotary_tables(positions):
    index = jnp.arange(HD // 2, dtype=f32)
    inverse = rope_base ** (-2.0 * index / HD)
    angles = positions[:, None] * inverse[None, :]
    cosine, sine = jnp.cos(angles), jnp.sin(angles)
    return jnp.tile(cosine, (1, 4)), jnp.concatenate([-sine, sine, -sine, sine], axis=1)


def local(
    hidden, cotangent, lengths, norm1_gain, w_z, w_x, w_shared, w_dt, dt_bias, a_log, d_skip,
    conv_w, conv_b, gated_gain, w_out, w_q, w_o, norm2_gain, w_gate, w_up, w_down,
):
    t = hidden.shape[1]
    shards = lax.axis_size("shard")
    tp, c = lax.axis_index("tp"), lax.axis_index("ctx")
    kv_rank = tp * (NQ // TP) // (NQ // KV)
    hid, cot = hidden[0], cotangent[0]

    def cut(v, start, size, axis):
        return lax.dynamic_slice_in_dim(v, start, size, axis)

    key_start = 2 * N + kv_rank * HD
    dt_cols = cut(w_dt, tp * HL, HL, 1)
    rows = w_z.shape[0]
    misc = [
        dt_cols,
        jnp.zeros((rows, GAIN_COL - HL), bf16),
        norm1_gain[:, None],
        norm2_gain[:, None],
        jnp.zeros((rows, 128 - GAIN_COL - 2), bf16),
    ]
    wa = jnp.concatenate(
        [
            w_z,
            w_x,
            w_shared[:, : 2 * N],
            w_q,
            cut(w_shared, key_start, HD, 1),
            cut(w_shared, key_start + KV * HD, HD, 1),
        ]
        + misc,
        axis=1,
    )
    wb = jnp.concatenate([w_out.T, w_o.T, w_gate, w_up, w_down.T], axis=1)
    taps = jnp.concatenate([conv_w, conv_b[None], jnp.zeros((3, DI + 2 * N), bf16)], axis=0)
    taps = jnp.concatenate([cut(taps, tp * WI, WI, 1), taps[:, DI:]], axis=1).astype(f32)
    bias = cut(dt_bias.astype(f32), tp * HL, HL, 0)
    rate = -jnp.exp(cut(a_log.astype(f32), tp * HL, HL, 0))
    prm = jnp.pad(jnp.stack([bias, rate]), ((0, 6), (0, 128 - HL)))
    skip = jnp.repeat(cut(d_skip.astype(f32), tp * HL, HL, 0), P_SIZE)
    gain_gate = cut(gated_gain.astype(f32), tp * WI, WI, 0)
    chan = jnp.pad(jnp.stack([gain_gate, skip]), ((0, 6), (0, 0)))
    cos, sin = rotary_tables((c * t + jnp.arange(t, dtype=jnp.int32)).astype(f32))

    wfull_a, normed, gains, z, cin, q, kv, dt = project(shards, hid, wa)
    (
        wfull_b, pre, hist, q_low, kk, vv, att, lse, lse_row, ssd, start, steps, cum, tot, gl, square,
    ) = forward(shards, cin, q, kv, dt, z, cos, sin, wb, taps, prm, chan, lengths)
    output, grad_own, grads, gain_two, total_square, ggl, grad_att, dots = ffn(
        hid, cot, gl, att.astype(bf16), square, wfull_b, gains, lengths
    )
    lin, grad_b, conv_grads, chan_grads, head_grads = backward(
        shards, ggl, grad_att, dots, total_square, grads, pre, cin, hist, q_low, kk, vv, att,
        lse_row, ssd, start, steps, cum, tot, dt, z, cos, sin, taps, prm, chan, lengths,
    )
    grad_hidden, grad_a, shared = finish(
        shards, lin, normed, wfull_a, hid, grad_own, gains, gain_two
    )

    def place(v, width, start, axis=0):
        shape = list(v.shape)
        shape[axis] = width
        return lax.dynamic_update_slice_in_dim(jnp.zeros(shape, f32), v, start, axis)

    conv_full = place(conv_grads[:5, :WI], DI, tp * WI, 1)
    conv_full = jnp.concatenate([conv_full, conv_grads[:5, WI:]], axis=1).reshape(-1)
    gate_full = place(chan_grads[0], DI, tp * WI)
    heads = place(head_grads[:3, :HL], H, tp * HL, 1).reshape(-1)
    small = lax.psum(jnp.concatenate([conv_full, gate_full, heads]), ("shard", "ctx", "tp"))
    width = DI + 2 * N
    conv_all = small[: 5 * width].reshape(5, width)
    gate_all = small[5 * width : 5 * width + DI]
    head_all = small[5 * width + DI :].reshape(3, H)

    maps = shared.sum(0)
    first, second = shared[0] + shared[1], shared[2] + shared[3]
    grad_shared = jnp.concatenate(
        [
            maps[:, : 2 * N],
            first[:, 256 : 256 + HD],
            second[:, 256 : 256 + HD],
            first[:, 256 + HD : 384],
            second[:, 256 + HD : 384],
        ],
        axis=1,
    )
    grad_dt = jnp.concatenate([shared[i, :, 384 : 384 + HL] for i in range(TP)], axis=1)
    return (
        output[None],
        grad_hidden[None],
        maps[:, 384 + GAIN_COL],
        grad_a[:, CZ:CX],
        grad_a[:, CX:CM],
        grad_shared,
        grad_dt,
        head_all[0],
        head_all[1],
        head_all[2],
        conv_all[:4],
        conv_all[4],
        gate_all,
        grad_b[:, CO:CW].T,
        grad_a[:, CQ:CK],
        grad_b[:, CW:CG].T,
        maps[:, 384 + GAIN_COL + 1],
        grad_b[:, CG:CU],
        grad_b[:, CU:CD],
        grad_b[:, CD:CB].T,
    )


def solution(mesh):
    placed = (
        P("shard", "ctx", None),
        P("shard", "ctx", None),
        P("shard"),
        P(("shard", "ctx")),
        P(("shard", "ctx"), "tp"),
        P(("shard", "ctx"), "tp"),
        P(("shard", "ctx"), None),
        P(("shard", "ctx"), None),
        P(),
        P(),
        P(),
        P(),
        P(),
        P(),
        P("tp", ("shard", "ctx")),
        P(("shard", "ctx"), "tp"),
        P("tp", ("shard", "ctx")),
        P(("shard", "ctx")),
        P(("shard", "ctx"), "tp"),
        P(("shard", "ctx"), "tp"),
        P("tp", ("shard", "ctx")),
    )
    return jax.shard_map(
        local,
        mesh=mesh,
        in_specs=placed,
        out_specs=(
            P("shard", "ctx", "tp"),
            P("shard", "ctx", None),
            P(("shard", "ctx", "tp")),
            P(("shard", "ctx"), "tp"),
            P(("shard", "ctx"), "tp"),
            P(("shard", "ctx", "tp"), None),
            P(("shard", "ctx", "tp"), None),
            P(),
            P(),
            P(),
            P(),
            P(),
            P(),
            P("tp", ("shard", "ctx")),
            P(("shard", "ctx"), "tp"),
            P("tp", ("shard", "ctx")),
            P(("shard", "ctx", "tp")),
            P(("shard", "ctx"), "tp"),
            P(("shard", "ctx"), "tp"),
            P("tp", ("shard", "ctx")),
        ),
        check_vma=False,
    )
```

time: 1520 us -> 491 us (0.32)
  waiting for transfers between devices: 806 us -> 0 us
  Pallas kernels: 0 us -> 393 us
  matrix products: 203 us -> 0 us
  other arithmetic: 157 us -> 9.74 us
  blocking collectives: 184 us -> 48.6 us
  local copies, waits for them, and re-layouts: 132 us -> 28.9 us
  between operations: 18.9 us -> 2.24 us
    pallas_call x0 -> x5, Pallas kernels: none -> 393 us  [the longest x1 134 us: ffn(): pl.pallas_call(ffn_kernel, out_shape=[jax.ShapeDtypeStruct(*o) for o in o...]
    reduce_scatter x12 -> x0, waiting for transfers between devices: 371 us -> none  [the longest x1 138 us: local(): lax.psum_scatter(grad_shared, ('shard', 'ctx', 'tp'), scatter_dimension=0...]
    psum x3 -> x0, waiting for transfers between devices: 320 us -> none  [the longest x1 150 us: local(): lax.psum((project_part, attn_part, square_part), 'tp')]
    dot_general x59 -> x0, matrix products: 197 us -> none  [the longest x9 32.9 us: matmul_tn(): lax.dot_general(lhs_matrix, rhs_matrix, (((0,), (0,)), ((), ())), preferr...]
    all_gather x13 -> x0, blocking collectives: 124 us -> none  [the longest x1 17.1 us: local(): lax.all_gather(w_z, ('shard', 'ctx'), axis=0, tiled=True)]
    all_gather x4 -> x0, waiting for transfers between devices: 58.4 us -> none  [the longest x1 21.3 us: local(): lax.all_gather(w_down, ('shard', 'ctx'), axis=1, tiled=True)]
    unnamed x21 -> x0, waiting for transfers between devices: 56.6 us -> none
    unnamed x4 -> x0, blocking collectives: 49.6 us -> none
  transfers between devices with their start and end apart: 20 -> 0, of which waited for: 15 -> 0; matrix products, arithmetic and copies ran while one was open for 19% -> 0% of each run, Pallas kernels for 0% -> 0%
where the time goes in v1:
time: 491 us; the launch traced here: 482 us
  Pallas kernels  393 us (80%)
  blocking collectives  48.6 us (10%)
  local copies, waits for them, and re-layouts  28.9 us (6%)
  other arithmetic  9.74 us (2%)
    pallas_call x1, Pallas kernels, ffn(): pl.pallas_call(ffn_kernel, out_shape=[jax.ShapeDtypeStruct(*o) for o in o...  134 us
    pallas_call x1, Pallas kernels, forward(): pl.pallas_call(functools.partial(forward_kernel, shards), out_shape=[jax....  73.1 us
    pallas_call x1, Pallas kernels, finish(): pl.pallas_call(functools.partial(finish_kernel, shards), out_shape=[jax.S...  72.7 us
    pallas_call x1, Pallas kernels, backward(): pl.pallas_call(functools.partial(backward_kernel, shards), out_shape=[jax...  70.9 us
    psum x1, blocking collectives, local(): lax.psum(jnp.concatenate([conv_full, gate_full, heads]), ('shard', 'ctx',...  48.6 us
    pallas_call x1, Pallas kernels, project(): pl.pallas_call(functools.partial(project_kernel, shards), out_shape=[jax....  41.4 us
    unnamed x42, local copies, waits for them, and re-layouts  10 us

profile of v1, /device:TPU:0, one launch (start us, length us, event | category | flops | bytes accessed | tf_op | source)
XLA Modules:
  0.0 482.1 jit_solution(6146124375617707590)
XLA Ops:
  0.8 0.9 constant_dynamic-slice_fusion.2
  1.7 0.1 copy.78
  1.8 0.8 slice.121
  2.6 0.8 copy.65
  3.4 0.8 copy.66
  4.2 1.8 concatenate.27.wa
  6.0 41.4 %project.1 = (bf16[1024,1408]{1,0:T(8,128)(2,1)}, bf16[1024,1024]{1,0:T(8,128)(2,1)}, f32[8,1024]{1,0:T(8,128)}, f32[1024,384]{1,0:T(8,128)}, bf16[1024,640]{1,0...) custom-call(bf16[1024,1024]{1,0:T(8,128)(2,1)} %bitcast.35, ...), custom_call_target="tpu_custom_call" | custom-call | tf_op jit(solution)/shard_map/project/pallas_call | solution.py:297
  47.4 0.8 dynamic-slice_convert_fusion
  48.4 0.6 select_maximum_fusion.chan
  49.2 0.6 select_maximum_fusion.1.prm
  49.9 0.6 maximum_convert_fusion.taps
  50.6 1.9 fusion
  52.5 1.3 pad_maximum_fusion.sin
  53.8 0.2 copy.68
  54.0 1.0 copy.72.cos
  55.7 0.1 copy.69
  55.9 0.1 copy.70
  56.1 0.1 copy.71
  56.2 0.8 copy-done.2
  57.0 73.1 %mix_forward.1 = (bf16[1024,2048]{1,0:T(8,128)(2,1)}, f32[1024,640]{1,0:T(8,128)}, f32[8,640]{1,0:T(8,128)}, bf16[1024,128]{1,0:T(8,128)(2,1)}, bf16[2,1024,128]...) custom-call(bf16[1024,640]{1,0:T(8,128)(2,1)} %get-tuple-element.59., ...), custom_call_target="tpu_custom_call" | custom-call | tf_op jit(solution)/shard_map/mix_forward/pallas_call | solution.py:508
  130.1 1.8 convert_element_type.35.att
  131.9 134.5 %feed_forward.1 = (bf16[1024,256]{1,0:T(8,128)(2,1)}, f32[256,1024]{1,0:T(8,128)}, bf16[1024,2048]{1,0:T(8,128)(2,1)}, f32[8,1024]{1,0:T(8,128)}, f32[8,1024]{1,...) custom-call(bf16[1024,1024]{1,0:T(8,128)(2,1)} %bitcast.36, ...), custom_call_target="tpu_custom_call" | custom-call | tf_op jit(solution)/shard_map/feed_forward/pallas_call | solution.py:769
  266.4 70.9 %mix_backward.1 = (bf16[1024,1408]{1,0:T(8,128)(2,1)}, f32[128,2048]{1,0:T(8,128)}, f32[8,640]{1,0:T(8,128)}, f32[8,384]{1,0:T(8,128)}, f32[8,128]{1,0:T(8,128)}) custom-call(f32[1024,384]{1,0:T(8,128)} %get-tuple-element.70.ggl, bf16[1024,128]{1,0:T(8,128)(2,1)} %get-tuple-element.71.grad_att, f32[8,1024]{1,0:T(8,128)} %get-tuple-element.72.dots_in, ...), custom_call_target="tpu_custom_call" | custom-call | tf_op jit(solution)/shard_map/mix_backward/pallas_call | solution.py:1061
  337.3 0.7 slice_dynamic-update-slice_fusion
  338.0 0.7 slice.140
  338.7 0.7 slice_reduce_fusion.2
  339.4 0.3 dynamic_update_slice.10
  339.7 0.7 slice.142
  340.6 48.6 %psum.7 = f32[10568]{0:T(1024)S(1)} all-reduce(f32[10568]{0:T(1024)S(1)} %pad_maximum_fusion.2), channel_id=1, replica_groups=mesh['shard'=4,'ctx'=2,'tp'=4] {'shard','ctx','tp'}, use_global_device_ids=true, to_apply=%region_1.2 | all-reduce | flops 10568 | bytes 84544 | tf_op jit(solution)/shard_map/psum | solution.py:1312
  389.2 0.6 slice.147
  389.9 0.6 slice.168
  390.5 0.6 slice.169
  391.1 0.6 fusion.4
  391.6 72.7 %project_backward.1 = (f32[1024,1024]{1,0:T(8,128)}, f32[128,1280]{1,0:T(8,128)}, f32[4,32,512]{2,1,0:T(8,128)}) custom-call(bf16[1024,1408]{1,0:T(8,128)(2,1)} %get-tuple-element.86.lin, bf16[1024,1024]{1,0:T(8,128)(2,1)} %get-tuple-element.87.normed, bf16[1024,1408]{1,0:T(8,128)(2,1)} %get-tuple-element.88.wfull, bf16[1024,1024]{1,0:T(8,128)(2,1)} %bitcast.37, ...), custom_call_target="tpu_custom_call" | custom-call | tf_op jit(solution)/shard_map/project_backward/pallas_call | solution.py:1208
  464.4 0.9 slice_bitcast_fusion.6
  465.4 0.7 copy.74
  466.0 1.0 add_bitcast_fusion
  467.1 1.0 reduce_sum.9
  468.1 0.7 concatenate.32
  468.8 1.8 fusion.1
  470.6 0.7 slice_reduce_fusion
  471.3 1.5 slice.151
  472.8 0.8 slice_bitcast_fusion
  473.6 0.8 copy.77
  474.5 0.8 copy.75
  475.3 0.7 copy.76
  476.0 0.8 copy.89
  476.8 4.8 copy.90
  (66 shorter events, 1.2 us)
Async XLA Ops:
  0.7 1.0 copy-start
  0.7 47.5 %copy-start.11 = (bf16[24]{0:T(256)(128)(2,1)S(1)}, bf16[24]{0:T(256)(128)(2,1)}, u32[]{:S(2)}) copy-start(bf16[24]{0:T(256)(128)(2,1)} %param.31) | copy-start | bytes 148
  0.7 48.4 %copy-start.12 = (bf16[24]{0:T(256)(128)(2,1)S(1)}, bf16[24]{0:T(256)(128)(2,1)}, u32[]{:S(2)}) copy-start(bf16[24]{0:T(256)(128)(2,1)} %param.29) | copy-start | bytes 148
  0.7 48.4 %copy-start.13 = (bf16[24]{0:T(256)(128)(2,1)S(1)}, bf16[24]{0:T(256)(128)(2,1)}, u32[]{:S(2)}) copy-start(bf16[24]{0:T(256)(128)(2,1)} %param.30) | copy-start | bytes 148
  0.7 49.1 %copy-start.10 = (bf16[1792]{0:T(1024)(128)(2,1)S(1)}, bf16[1792]{0:T(1024)(128)(2,1)}, u32[]{:S(2)}) copy-start(bf16[1792]{0:T(1024)(128)(2,1)} %param.33) | copy-start | bytes 10756
  0.7 49.1 %copy-start.9 = (bf16[4,1792]{1,0:T(4,128)(2,1)S(1)}, bf16[4,1792]{1,0:T(4,128)(2,1)}, u32[]{:S(2)}) copy-start(bf16[4,1792]{1,0:T(4,128)(2,1)} %param.32) | copy-start | bytes 43012
  50.6 5.1 %copy-start.7 = (bf16[384,128]{1,0:T(8,128)(2,1)S(1)}, bf16[384,128]{1,0:T(8,128)(2,1)}, u32[]{:S(2)}) copy-start(bf16[384,128]{1,0:T(8,128)(2,1)} %param.35) | copy-start | bytes 294916
  50.6 5.3 %copy-start.8 = (bf16[128,128]{1,0:T(8,128)(2,1)S(1)}, bf16[128,128]{1,0:T(8,128)(2,1)}, u32[]{:S(2)}) copy-start(bf16[128,128]{1,0:T(8,128)(2,1)} %param.37) | copy-start | bytes 98308
  52.5 3.5 copy-start.4
  52.5 3.5 copy-start.5
  52.5 3.5 copy-start.6
  56.2 0.8 copy-start.2
  464.4 8.4 %copy-start.1 = (f32[128,2048]{1,0:T(8,128)S(1)}, f32[128,2048]{1,0:T(8,128)}, u32[]{:S(2)}) copy-start(f32[128,2048]{1,0:T(8,128)} %get-tuple-element.97) | copy-start | bytes 3145732
  465.3 10.7 %copy-start.3 = (bf16[1024,256]{1,0:T(8,128)(2,1)S(1)}, bf16[1024,256]{1,0:T(8,128)(2,1)}, u32[]{:S(2)}) copy-start(bf16[1024,256]{1,0:T(8,128)(2,1)} %get-tuple-element.69) | copy-start | bytes 1572868
